TPU v7x, 32 devices: a whole 2x2x4 slice. The times are simulated.
32 devices in a mesh: segment: 8 (over z, y), tp: 4 (over x, core).
Axes of the slice: x: 2, y: 2, z: 4, core: 2. Of those that a mesh axis runs over, the one named last changes fastest.
Arguments:
- residual: bfloat16 [8, 128, 4096], P('segment', 'tp'), may hold values from -6 to 6
- pending: bfloat16 [8, 128, 4096], P('segment', 'tp'), may hold values from -6 to 6
- span_index: int32 [8], P('segment'), may hold values from 0 to 63
- prefix_len: int32 [8], P('segment'), may hold values from 192 to 1536
- norm_gain: bfloat16 [8, 4096], P('segment'), may hold values from 0.099609375 to 1.8984375
- w_query: bfloat16 [8, 4096, 4096], P('segment', None, 'tp'), may hold values from -0.1875 to 0.1875
- w_kv: bfloat16 [8, 4096, 1024], P('segment', None, 'tp'), may hold values from -0.09375 to 0.09375
- w_out: bfloat16 [8, 4096, 4096], P('segment', 'tp'), may hold values from -0.5 to 0.5
- prefix_cache: bfloat16 [8, 6144, 256], P('segment', 'tp'), may hold values from -68 to 68
Outputs:
- carried: bfloat16 [8, 128, 4096], P('segment', 'tp')
- output: bfloat16 [8, 128, 4096], P('segment', 'tp')
All inputs are finite; a program needn't handle non-finite values.
Results may differ from a plain program's by a relative error of at most 0.04.
Values may be sent and summed in bfloat16 or wider, within the bound.
A program may use at most 64 MiB of HBM per device.

v0:
```python
import jax
import jax.numpy as jnp
from jax import lax
from jax.sharding import PartitionSpec as P

KV_HEADS = 4
HD = 128
SPAN = 128
PREFIX = 1536
TICKS = 2


norm_eps = 1e-05
rope_base = 500000.0


def from_partner(array, axis, stride):
    return lax.ppermute(array, axis, [(i, i ^ 1 << stride) for i in range(lax.axis_size(axis))])


def shifted(block, axis, distance):
    devices = range(lax.axis_size(axis))
    route = [(i - distance, i) for i in devices if i - distance in devices]
    return lax.ppermute(block, axis, route)


def rotate(values, positions):
    half_width = values.shape[-1] // 2
    inverse = rope_base ** (
        -jnp.arange(0, values.shape[-1], 2, dtype=jnp.float32) / values.shape[-1]
    )
    angles = positions.astype(jnp.float32)[:, None] * inverse[None, :]
    cosine_table = jnp.cos(angles)[:, None, :]
    sine_table = jnp.sin(angles)[:, None, :]
    first_half = values[..., :half_width]
    second_half = values[..., half_width:]
    return jnp.concatenate(
        [
            first_half * cosine_table - second_half * sine_table,
            second_half * cosine_table + first_half * sine_table,
        ],
        axis=-1,
    )


def shards(
    residual, pending, span_index, prefix_len, norm_gain, w_query, w_kv, w_out, prefix_cache
):
    group_size = lax.axis_size("tp") // KV_HEADS
    group_bits = group_size.bit_length() - 1
    tp_place = lax.axis_index("tp")
    local_heads = w_query.shape[2] // HD
    weight_query = w_query[0]
    weight_pairs = w_kv[0]
    weight_out = w_out[0]
    query_width = weight_query.shape[1]
    gain_row = norm_gain[0].astype(jnp.float32)
    head_cache = prefix_cache[0]
    for bit_number in range(group_bits):
        partner = from_partner(head_cache, "tp", bit_number)
        lower_half = tp_place // (1 << bit_number) % 2 == 0
        head_cache = jnp.where(
            lower_half,
            jnp.concatenate([head_cache, partner], 0),
            jnp.concatenate([partner, head_cache], 0),
        )
    cache_keys = head_cache[:, :HD]
    cache_values = head_cache[:, HD:]
    slot_index = jnp.arange(PREFIX, dtype=jnp.int32)
    token_index = jnp.arange(SPAN, dtype=jnp.int32)
    causal = token_index[None, :] <= token_index[:, None]
    score_scale = HD ** (-0.5)
    rows_now = residual[0]
    pending_now = pending[0]
    index_now = span_index
    for segment_tick in range(TICKS):
        last_tick = segment_tick + 1 == TICKS
        widths = rows_now.astype(jnp.float32)
        mean_square = jnp.mean(widths * widths, axis=-1, keepdims=True)
        normed = (widths * lax.rsqrt(mean_square + norm_eps) * gain_row).astype(jnp.bfloat16)
        carried = (widths + pending_now.astype(jnp.float32)).astype(jnp.bfloat16)
        block_rows = lax.all_gather(normed, "tp", axis=0, tiled=True)
        projected = jnp.concatenate(
            [
                jnp.dot(block_rows, weight_query, preferred_element_type=jnp.float32),
                jnp.dot(block_rows, weight_pairs, preferred_element_type=jnp.float32),
            ],
            axis=1,
        )
        positions = index_now[0] * SPAN + token_index
        queries = rotate(
            projected[:, :query_width].reshape(SPAN, local_heads, HD), positions
        ).astype(jnp.bfloat16)
        fresh_head = projected[:, query_width:].astype(jnp.bfloat16)
        for bit_number in range(group_bits):
            partner = from_partner(fresh_head, "tp", bit_number)
            lower_half = tp_place // (1 << bit_number) % 2 == 0
            fresh_head = jnp.where(
                lower_half,
                jnp.concatenate([fresh_head, partner], 1),
                jnp.concatenate([partner, fresh_head], 1),
            )
        new_keys = rotate(fresh_head[:, None, :HD].astype(jnp.float32), positions)[:, 0, :].astype(
            jnp.bfloat16
        )
        new_values = fresh_head[:, HD:]
        score_prefix = (
            jnp.einsum("chd,pd->hcp", queries, cache_keys, preferred_element_type=jnp.float32)
            * score_scale
        )
        score_span = (
            jnp.einsum("chd,kd->hck", queries, new_keys, preferred_element_type=jnp.float32)
            * score_scale
        )
        score_prefix = jnp.where(
            (slot_index < prefix_len[0])[None, None, :], score_prefix, -jnp.inf
        )
        score_span = jnp.where(causal[None], score_span, -jnp.inf)
        row_peak = jnp.maximum(
            jnp.max(score_prefix, axis=-1, keepdims=True),
            jnp.max(score_span, axis=-1, keepdims=True),
        )
        exp_prefix = jnp.exp(score_prefix - row_peak)
        exp_span = jnp.exp(score_span - row_peak)
        denominator = jnp.sum(exp_prefix, axis=-1, keepdims=True) + jnp.sum(
            exp_span, axis=-1, keepdims=True
        )
        weight_prefix = (exp_prefix / denominator).astype(jnp.bfloat16)
        weight_span = (exp_span / denominator).astype(jnp.bfloat16)
        attended = jnp.einsum(
            "hcp,pd->chd", weight_prefix, cache_values, preferred_element_type=jnp.float32
        )
        attended = attended + jnp.einsum(
            "hck,kd->chd", weight_span, new_values, preferred_element_type=jnp.float32
        )
        attended = attended.astype(jnp.bfloat16).reshape(SPAN, local_heads * HD)
        summed = lax.psum_scatter(
            jnp.dot(attended, weight_out, preferred_element_type=jnp.float32),
            "tp",
            scatter_dimension=0,
            tiled=True,
        )
        output = summed.astype(jnp.bfloat16)
        if not last_tick:
            rows_now, pending_now, index_now = shifted((carried, output, index_now), "segment", 1)
    return (carried[None], output[None])


def solution(mesh):
    in_specs = (
        P("segment", "tp", None),
        P("segment", "tp", None),
        P("segment"),
        P("segment"),
        P("segment", None),
        P("segment", None, "tp"),
        P("segment", None, "tp"),
        P("segment", "tp", None),
        P("segment", "tp", None),
    )
    out_specs = (P("segment", "tp", None), P("segment", "tp", None))
    return jax.shard_map(shards, mesh=mesh, in_specs=in_specs, out_specs=out_specs, check_vma=False)
```

profile of v0, /device:TPU:0, one launch (start us, length us, event | category | flops | bytes accessed | tf_op | source)
XLA Modules:
  0.0 144.5 jit_solution(4104048164658865915)
XLA Ops:
  7.2 0.9 mul.299
  8.1 1.1 fusion.39
  9.2 1.9 %fusion.38 = (bf16[32,4096]{1,0:T(8,128)(2,1)S(1)}, bf16[32,4096]{1,0:T(8,128)(2,1)}) fusion(bf16[1,32,4096]{2,1,0:T(8,128)(2,1)} %param.10, bf16[1,32,4096]{2,1,0:T(8,128)(2,1)} %param.9, f32[4096]{0:T(1024)S(1)} %bitcast.150, f32[32]{0:T(128)S(1)} %add_rsqrt_fusion.1), kind=kLoop, calls=%fused_computation.52 | loop fusion | flops 917504 | bytes 1065088 | tf_op jit(solution)/shard_map/convert_element_type | solution.py:81
  11.2 4.9 %collective-permute-start = (bf16[32,4096]{1,0:T(8,128)(2,1)S(1)}, bf16[32,4096]{1,0:T(8,128)(2,1)S(1)}, u32[]{:S(2)}, u32[]{:S(2)}) collective-permute-start(bf16[32,4096]{1,0:T(8,128)(2,1)S(1)} %get-tuple-element.10), channel_id=1, source_target_pairs={{0,4},{4,8},{8,12},{12,16},{16,20},{20,24},{24,28},{1,5},{5,9},{9,... | collective-permute-start | bytes 786440 | tf_op jit(solution)/shard_map/ppermute | solution.py:24
  16.1 4.0 %collective-permute-start.2 = (s32[1]{0:T(128)}, s32[1]{0:T(128)}, u32[]{:S(2)}, u32[]{:S(2)}) collective-permute-start(s32[1]{0:T(128)} %param.11), channel_id=1, source_target_pairs={{0,4},{4,8},{8,12},{12,16},{16,20},{20,24},{24,28},{1,5},{5,9},{9,... | collective-permute-start | bytes 20 | tf_op jit(solution)/shard_map/ppermute | solution.py:24
  21.8 0.8 fusion.37
  22.7 11.3 %copy.53 = bf16[1024,4096]{1,0:T(8,128)(2,1)} copy(bf16[1024,4096]{0,1:T(8,128)(2,1)} %bitcast.143) | data formatting | bytes 16777216 | tf_op jit(solution)/shard_map/dot_general | solution.py:85
  34.7 0.3 multiply_cosine_fusion.1
  35.1 2.1 %fusion.24 = bf16[128,256]{0,1:T(8,128)(2,1)S(1)} fusion(bf16[128,4096]{1,0:T(8,128)(2,1)} %all-gather.3.cloned.1.call-done, bf16[1,4096,256]{2,1,0:T(8,128)(2,1)S(1)} %copy-done), kind=kOutput, calls=%fused_computation.36 | convolution fusion | flops 268468224 | bytes 3211264 | tf_op jit(solution)/shard_map/dot_general | solution.py:86
  37.2 6.4 %fusion.32 = f32[128,8,128]{0,2,1:T(8,128)S(1)} fusion(bf16[8,128,4096]{2,1,0:T(8,128)(2,1)} %bitcast.139, bf16[128,4096]{1,0:T(8,128)(2,1)} %all-gather.3.cloned.1.call-done), kind=kOutput, calls=%fused_computation.40 | convolution fusion | flops 1073741824 | bytes 9961472 | tf_op jit(solution)/shard_map/dot_general | solution.py:85
  43.7 5.9 %all-gather.5.cloned.1.call-done = bf16[128,4096]{1,0:T(8,128)(2,1)} async-done(((bf16[32,4096]{1,0:T(8,128)(2,1)}), bf16[128,4096]{1,0:T(8,128)(2,1)}) %all-gather.5.cloned.1.call-update) | async-done | bytes 1048592 | tf_op jit(solution)/shard_map/all_gather | solution.py:82
  49.6 2.1 %fusion.27 = bf16[128,256]{0,1:T(8,128)(2,1)S(1)} fusion(bf16[128,4096]{1,0:T(8,128)(2,1)} %all-gather.5.cloned.1.call-done, bf16[1,4096,256]{2,1,0:T(8,128)(2,1)S(1)} %copy-done), kind=kOutput, calls=%fused_computation.37 | convolution fusion | flops 268468224 | bytes 3211264 | tf_op jit(solution)/shard_map/dot_general | solution.py:86
  51.8 0.3 fusion.64
  52.1 6.1 %fusion.30 = f32[128,8,128]{0,2,1:T(8,128)S(1)} fusion(bf16[8,128,4096]{2,1,0:T(8,128)(2,1)} %bitcast.140, bf16[128,4096]{1,0:T(8,128)(2,1)} %all-gather.5.cloned.1.call-done), kind=kOutput, calls=%fused_computation.38 | convolution fusion | flops 1073741824 | bytes 9961472 | tf_op jit(solution)/shard_map/dot_general | solution.py:85
  58.4 1.0 fusion.45
  59.4 1.8 %bitcast_reduce_fusion = (f32[8,128]{1,0:T(8,128)S(1)}, f32[8,128]{1,0:T(8,128)S(1)}, f32[128,8,1536]{2,0,1:T(8,128)S(1)}) fusion(pred[1536]{0:T(1024)(128)(4,1)S(1)} %iota_compare_fusion.1, f32[128,8,1536]{2,0,1:T(8,128)S(1)} %fusion.45, bf16[1536,256]{1,0:T(8,128)(2,1)S(1)} %bitcast.146, bf16[128,8,64]{0,2,1:T(8,128)(2,1)S(1)} %get-tuple-element.7, ...), kind=kOutput, calls=%fused_computation.5 | convolution fusion | flops 412612608 | bytes 13248512 | tf_op jit(solution)/shard_map/chd,pd->hcp/dot_general | solution.py:108
  61.2 0.3 fusion.81
  61.5 0.3 fusion.82
  61.9 2.9 %fusion.7 = (f32[8,128]{1,0:T(8,128)S(1)}, f32[8,128]{1,0:T(8,128)S(1)}) fusion(f32[128,8,1536]{2,0,1:T(8,128)S(1)} %get-tuple-element.24, f32[8,128]{1,0:T(8,128)S(1)} %max.17, pred[1536]{0:T(1024)(128)(4,1)S(1)} %iota_compare_fusion.1, f32[8,128]{1,0:T(8,128)S(1)} %max.16, f32[128,8,1536]{2,0,1:T(8,128)S(1)} %fusion.45), kind=kLoop, calls=%fused_computation.15 | loop fusion | flops 12580864 | bytes 12600832 | tf_op jit(solution)/shard_map/reduce_sum | solution.py:125
  64.8 1.8 %fusion.15 = f32[128,8,128]{0,2,1:T(8,128)S(1)} fusion(f32[128,8,1536]{2,0,1:T(8,128)S(1)} %fusion.45, f32[8,128]{1,0:T(8,128)S(1)} %add.86, f32[8,128]{1,0:T(8,128)S(1)} %max.16, pred[1536]{0:T(1024)(128)(4,1)S(1)} %iota_compare_fusion.1, bf16[1536,256]{1,0:T(8,128)(2,1)S(1)} %bitcast.147), kind=kOutput, calls=%fused_computation.23 | convolution fusion | flops 410517504 | bytes 7219200 | tf_op jit(solution)/shard_map/hcp,pd->chd/dot_general | solution.py:130
  66.6 0.3 fusion.22
  66.9 0.3 slice-done.1
  67.2 2.6 %fusion.2 = f32[128,4096]{1,0:T(8,128)} fusion(bf16[128,1024]{0,1:T(8,128)(2,1)S(1)} %bitcast.148, bf16[1,1024,4096]{2,1,0:T(8,128)(2,1)S(1)} %bitcast.142), kind=kOutput, calls=%fused_computation.2 | convolution fusion | flops 1073741824 | bytes 10747904 | tf_op jit(solution)/shard_map/dot_general | solution.py:138
  70.0 4.0 %fusion.14 = f32[128,8,128]{0,2,1:T(8,128)S(1)} fusion(f32[128,8,1536]{2,0,1:T(8,128)} %copy-done.1, f32[8,128]{1,0:T(8,128)S(1)} %add.94, f32[8,128]{1,0:T(8,128)S(1)} %max.17, pred[1536]{0:T(1024)(128)(4,1)S(1)} %iota_compare_fusion.1, bf16[1536,256]{1,0:T(8,128)(2,1)} %bitcast.144), kind=kOutput, calls=%fused_computation.22 | convolution fusion | flops 410517504 | bytes 7218688 | tf_op jit(solution)/shard_map/hcp,pd->chd/dot_general | solution.py:130
  74.0 0.3 fusion.23
  74.3 6.7 %fusion = f32[128,4096]{1,0:T(8,128)} fusion(bf16[128,1024]{0,1:T(8,128)(2,1)S(1)} %bitcast.149, bf16[1,1024,4096]{2,1,0:T(8,128)(2,1)} %param.16), kind=kOutput, calls=%fused_computation | convolution fusion | flops 1073741824 | bytes 10747904 | tf_op jit(solution)/shard_map/dot_general | solution.py:138
  81.0 20.5 %reduce-scatter.3.cloned.1.call-done = f32[32,4096]{1,0:T(8,128)} async-done(((f32[128,4096]{1,0:T(8,128)}), f32[32,4096]{1,0:T(8,128)}) %reduce-scatter.3.cloned.1.call-update) | async-done | bytes 524304 | tf_op jit(solution)/shard_map/reduce_scatter | solution.py:137
  101.5 1.1 convert_element_type.115
  102.5 3.4 %collective-permute-start.1 = (bf16[32,4096]{1,0:T(8,128)(2,1)S(1)}, bf16[32,4096]{1,0:T(8,128)(2,1)S(1)}, u32[]{:S(2)}, u32[]{:S(2)}) collective-permute-start(bf16[32,4096]{1,0:T(8,128)(2,1)S(1)} %convert_element_type.115), channel_id=1, source_target_pairs={{0,4},{4,8},{8,12},{12,16},{16,20},{20,24},{24,28},{1,5},{5,9},{9,... | collective-permute-start | bytes 786440 | tf_op jit(solution)/shard_map/ppermute | solution.py:24
  105.9 29.5 %reduce-scatter.5.cloned.1.call-done = f32[32,4096]{1,0:T(8,128)} async-done(((f32[128,4096]{1,0:T(8,128)}), f32[32,4096]{1,0:T(8,128)}) %reduce-scatter.5.cloned.1.call-update) | async-done | bytes 524304 | tf_op jit(solution)/shard_map/reduce_scatter | solution.py:137
  135.5 1.8 %convert_bitcast_fusion = bf16[1,32,4096]{2,1,0:T(8,128)(2,1)} fusion(f32[32,4096]{1,0:T(8,128)} %reduce-scatter.5.cloned.1.call-done), kind=kLoop, calls=%fused_computation.69 | loop fusion | flops 131072 | bytes 786432 | tf_op jit(solution)/shard_map/broadcast_in_dim | solution.py:146
  137.2 0.8 fusion.46
  (39 shorter events, 1.1 us)
Async XLA Ops:
  7.2 27.9 %copy-start = (bf16[1,4096,256]{2,1,0:T(8,128)(2,1)S(1)}, bf16[1,4096,256]{2,1,0:T(8,128)(2,1)}, u32[]{:S(2)}) copy-start(bf16[1,4096,256]{2,1,0:T(8,128)(2,1)} %param.15) | copy-start | bytes 6291460
  7.2 27.9 %all-gather.3.cloned.1.call-start = ((), (), s32[]{:S(2)}) async-start(), calls=%async_computation.2 | async-start | bytes 1310720 | tf_op jit(solution)/shard_map/all_gather | solution.py:82
  11.1 38.5 %all-gather.5.cloned.1.call-start = ((), (), s32[]{:S(2)}) async-start(), calls=%async_computation.4 | async-start | bytes 1310720 | tf_op jit(solution)/shard_map/all_gather | solution.py:82
  11.2 10.4 %collective-permute-start = (bf16[32,4096]{1,0:T(8,128)(2,1)S(1)}, bf16[32,4096]{1,0:T(8,128)(2,1)S(1)}, u32[]{:S(2)}, u32[]{:S(2)}) collective-permute-start(bf16[32,4096]{1,0:T(8,128)(2,1)S(1)} %get-tuple-element.10), channel_id=1, source_target_pairs={{0,4},{4,8},{8,12},{12,16},{16,20},{20,24},{24,28},{1,5},{5,9},{9,... | collective-permute-start | bytes 786440 | tf_op jit(solution)/shard_map/ppermute | solution.py:24
  16.1 18.0 %collective-permute-start.2 = (s32[1]{0:T(128)}, s32[1]{0:T(128)}, u32[]{:S(2)}, u32[]{:S(2)}) collective-permute-start(s32[1]{0:T(128)} %param.11), channel_id=1, source_target_pairs={{0,4},{4,8},{8,12},{12,16},{16,20},{20,24},{24,28},{1,5},{5,9},{9,... | collective-permute-start | bytes 20 | tf_op jit(solution)/shard_map/ppermute | solution.py:24
  22.6 78.8 %reduce-scatter.3.cloned.1.call-start = ((), (), s32[]{:S(2)}) async-start(), calls=%async_computation.3 | async-start | bytes 2621440 | tf_op jit(solution)/shard_map/reduce_scatter | solution.py:137
  52.1 6.3 %copy-start.2 = (bf16[1,1536,256]{2,1,0:T(8,128)(2,1)S(1)}, bf16[1,1536,256]{2,1,0:T(8,128)(2,1)}, u32[]{:S(2)}) copy-start(bf16[1,1536,256]{2,1,0:T(8,128)(2,1)} %param.17) | copy-start | bytes 2359300
  61.2 3.6 %copy-start.1 = (f32[128,8,1536]{2,0,1:T(8,128)}, f32[128,8,1536]{2,0,1:T(8,128)S(1)}, u32[]{:S(2)}) copy-start(f32[128,8,1536]{2,0,1:T(8,128)S(1)} %get-tuple-element.24) | copy-start | bytes 18874372
  61.9 5.0 %slice-start = ((s8[8388608]{0:T(1024)(128)(4,1)}), s8[4194304]{0:T(1024)(128)(4,1)S(1)}, s32[]{:S(2)}) async-start(s8[8388608]{0:T(1024)(128)(4,1)} %bitcast.141), calls=%async_computation.6 | async-start | bytes 8388608
  64.8 2.4 %slice-start.1 = ((s8[8388608]{0:T(1024)(128)(4,1)}), s8[4194304]{0:T(1024)(128)(4,1)S(1)}, s32[]{:S(2)}) async-start(s8[8388608]{0:T(1024)(128)(4,1)} %bitcast.141), calls=%async_computation.7 | async-start | bytes 8388608
  69.8 65.6 %reduce-scatter.5.cloned.1.call-start = ((), (), s32[]{:S(2)}) async-start(), calls=%async_computation.5 | async-start | bytes 2621440 | tf_op jit(solution)/shard_map/reduce_scatter | solution.py:137
  102.5 34.7 %collective-permute-start.1 = (bf16[32,4096]{1,0:T(8,128)(2,1)S(1)}, bf16[32,4096]{1,0:T(8,128)(2,1)S(1)}, u32[]{:S(2)}, u32[]{:S(2)}) collective-permute-start(bf16[32,4096]{1,0:T(8,128)(2,1)S(1)} %convert_element_type.115), channel_id=1, source_target_pairs={{0,4},{4,8},{8,12},{12,16},{16,20},{20,24},{24,28},{1,5},{5,9},{9,... | collective-permute-start | bytes 786440 | tf_op jit(solution)/shard_map/ppermute | solution.py:24
Sparse Core Ops, SparseCore 0:
  11.2 19.4 all-gather.2
  32.8 16.7 all-gather.4
  70.0 31.4 reduce-scatter.2
  104.0 31.4 reduce-scatter.4
where the time goes:
time: 145 us
  waiting for transfers between devices  56.3 us (39%)
  matrix products  35.8 us (25%)
  between operations  16 us (11%)
  starting transfers between devices  12.4 us (9%)
  other arithmetic  12.4 us (9%)
  local copies, waits for them, and re-layouts  11.6 us (8%)
    reduce_scatter x2, waiting for transfers between devices, shards(): lax.psum_scatter(jnp.dot(attended, weight_out, preferred_element_type=jnp...  50 us
    dot_general x2, matrix products, shards(): jnp.dot(block_rows, weight_query, preferred_element_type=jnp.float32)  12.5 us
    ppermute x3, starting transfers between devices, shifted(): return lax.ppermute(block, axis, route)  12.3 us
    dot_general x1, local copies, waits for them, and re-layouts, shards(): jnp.dot(block_rows, weight_query, preferred_element_type=jnp.float32)  11.3 us
    dot_general x2, matrix products, shards(): jnp.dot(attended, weight_out, preferred_element_type=jnp.float32)  9.32 us
    all_gather x2, waiting for transfers between devices, shards(): block_rows = lax.all_gather(normed, 'tp', axis=0, tiled=True)  5.95 us
    dot_general x2, matrix products, shards(): jnp.einsum('hcp,pd->chd', weight_prefix, cache_values, preferred_element_...  5.81 us
    dot_general x2, matrix products, shards(): jnp.dot(block_rows, weight_pairs, preferred_element_type=jnp.float32)  4.3 us
  transfers between devices with their start and end apart: 7, of which 4 were waited for; matrix products, arithmetic and copies ran while one was open for 24% of the time, Pallas kernels for 0%

commit v1 on v0

--- a/solution.py
+++ b/solution.py
@@ -1,6 +1,12 @@
+import functools
+import math
+
 import jax
 import jax.numpy as jnp
+import numpy as np
 from jax import lax
+from jax.experimental import pallas as pl
+from jax.experimental.pallas import tpu as pltpu
 from jax.sharding import PartitionSpec as P
 
 KV_HEADS = 4
@@ -146,6 +152,465 @@
     return (carried[None], output[None])
 
 
+TP = 4
+ROWS = SPAN // TP
+HALF = ROWS // 2
+OUT_CHUNKS = 4
+TILE = 256
+MASKED = -1e30
+
+
+def fused_kernel(
+    sections,
+    span_ref,
+    len_ref,
+    residual_ref,
+    pending_ref,
+    gain_ref,
+    inverse_ref,
+    w_query_hbm,
+    w_kv_hbm,
+    w_out_hbm,
+    cache_hbm,
+    carried_ref,
+    output_ref,
+    w_query,
+    w_kv,
+    w_out,
+    keys,
+    values,
+    tokens,
+    carried_own,
+    carried_in,
+    index_own,
+    index_in,
+    projected,
+    queries,
+    attended,
+    partial,
+    own_sum,
+    pair_send,
+    pair_recv,
+    far_send,
+    far_recv,
+    first_out,
+    out_in,
+    load_sem,
+    gather_send,
+    gather_recv,
+    shift_send,
+    shift_recv,
+    pair_send_sem,
+    pair_recv_sem,
+    far_send_sem,
+    far_recv_sem,
+    out_send_sem,
+    out_recv_sem,
+):
+    features = w_query.shape[0]
+    query_width = w_query.shape[1]
+    heads = query_width // HD
+    chunk = features // OUT_CHUNKS
+    seg = lax.axis_index("segment")
+    me = lax.axis_index("tp")
+    pair = me + 1 - 2 * lax.rem(me, 2)
+    far = lax.rem(me + 2, TP)
+    far_pair = lax.rem(pair + 2, TP)
+    has_prev = seg > 0
+    has_next = seg < sections - 1
+
+    loads = []
+    quarter = features // 4
+    for part in range(4):
+        span = pl.ds(part * quarter, quarter)
+        loads.append((w_query_hbm.at[0, span], w_query.at[span]))
+    loads.append((w_kv_hbm.at[0], w_kv))
+    loads.append((cache_hbm.at[0, :, pl.ds(0, HD)], keys.at[pl.ds(0, PREFIX)]))
+    loads.append((cache_hbm.at[0, :, pl.ds(HD, HD)], values.at[pl.ds(0, PREFIX)]))
+    quarter_out = query_width // 4
+    for part in range(4):
+        span = pl.ds(part * quarter_out, quarter_out)
+        loads.append((w_out_hbm.at[0, span], w_out.at[span]))
+    loads = [
+        pltpu.make_async_copy(source, target, load_sem.at[number])
+        for number, (source, target) in enumerate(loads)
+    ]
+    for load in loads:
+        load.start()
+
+    barrier = pltpu.get_barrier_semaphore()
+    for partner in (pair, far):
+        pl.semaphore_signal(barrier, inc=1, device_id={"tp": partner})
+
+    @pl.when(has_prev)
+    def _():
+        pl.semaphore_signal(barrier, inc=1, device_id={"segment": seg - 1})
+
+    @pl.when(has_next)
+    def _():
+        pl.semaphore_signal(barrier, inc=1, device_id={"segment": seg + 1})
+
+    gain = gain_ref[...].astype(jnp.float32)
+
+    def rows_of(rank, part=None):
+        if part is None:
+            return pl.ds(pl.multiple_of(rank * ROWS, ROWS), ROWS)
+        return pl.ds(pl.multiple_of(rank * ROWS + part * HALF, HALF), HALF)
+
+    def normed(rows):
+        widths = rows.astype(jnp.float32)
+        mean_square = jnp.mean(widths * widths, axis=-1, keepdims=True)
+        return (widths * lax.rsqrt(mean_square + norm_eps) * gain).astype(jnp.bfloat16)
+
+    def gather_copy(tick, leg, part):
+        rank = far if leg == 2 else me
+        block = tokens.at[tick, rows_of(rank, part)]
+        return pltpu.make_async_remote_copy(
+            src_ref=block,
+            dst_ref=block,
+            send_sem=gather_send.at[tick, leg, part],
+            recv_sem=gather_recv.at[tick, leg, part],
+            device_id={"tp": far if leg == 0 else pair},
+        )
+
+    def shift_copy(part):
+        rows = pl.ds(part * HALF, HALF)
+        return pltpu.make_async_remote_copy(
+            src_ref=carried_own.at[rows],
+            dst_ref=carried_in.at[rows],
+            send_sem=shift_send.at[part],
+            recv_sem=shift_recv.at[part],
+            device_id={"segment": seg + 1},
+        )
+
+    def index_copy():
+        return pltpu.make_async_remote_copy(
+            src_ref=index_own,
+            dst_ref=index_in,
+            send_sem=shift_send.at[2],
+            recv_sem=shift_recv.at[2],
+            device_id={"segment": seg + 1},
+        )
+
+    def pair_copy(tick, number):
+        return pltpu.make_async_remote_copy(
+            src_ref=pair_send.at[tick, number],
+            dst_ref=pair_recv.at[tick, number],
+            send_sem=pair_send_sem.at[tick, number],
+            recv_sem=pair_recv_sem.at[tick, number],
+            device_id={"tp": pair},
+        )
+
+    def far_copy(tick, number):
+        return pltpu.make_async_remote_copy(
+            src_ref=far_send.at[tick, number],
+            dst_ref=far_recv.at[tick, number],
+            send_sem=far_send_sem.at[tick, number],
+            recv_sem=far_recv_sem.at[tick, number],
+            device_id={"tp": far},
+        )
+
+    def out_copy(number):
+        return pltpu.make_async_remote_copy(
+            src_ref=first_out.at[number],
+            dst_ref=out_in.at[number],
+            send_sem=out_send_sem.at[number],
+            recv_sem=out_recv_sem.at[number],
+            device_id={"segment": seg + 1},
+        )
+
+    tokens[0, rows_of(me)] = normed(residual_ref[0])
+    carried_own[...] = (
+        residual_ref[0].astype(jnp.float32) + pending_ref[0].astype(jnp.float32)
+    ).astype(jnp.bfloat16)
+    index_own[...] = jnp.full(index_own.shape, span_ref[0], jnp.int32)
+
+    pl.semaphore_wait(barrier, 2 + has_prev.astype(jnp.int32) + has_next.astype(jnp.int32))
+
+    for part in range(2):
+        gather_copy(0, 0, part).start()
+
+    @pl.when(has_next)
+    def _():
+        for part in range(2):
+            shift_copy(part).start()
+        index_copy().start()
+
+    for part in range(2):
+        gather_copy(0, 1, part).start()
+
+    @pl.when(jnp.logical_not(has_prev))
+    def _():
+        carried_in[...] = jnp.zeros_like(carried_in)
+        index_in[...] = jnp.zeros_like(index_in)
+        out_in[...] = jnp.zeros_like(out_in)
+
+    lane = lax.broadcasted_iota(jnp.int32, (SPAN, HD), 1)
+    row = lax.broadcasted_iota(jnp.int32, (SPAN, HD), 0)
+
+    def tables(index_tile):
+        positions = (index_tile[0:1, :] * SPAN + row).astype(jnp.float32)
+        angles = positions * inverse_ref[0:1, :]
+        sine = jnp.sin(angles)
+        return jnp.cos(angles), jnp.where(lane < HD // 2, -sine, sine)
+
+    def rotated(block, table):
+        cosine, sine = table
+        return (block * cosine + pltpu.roll(block, HD // 2, 1) * sine).astype(jnp.bfloat16)
+
+    causal_bias = jnp.where(lane <= row, 0.0, MASKED).astype(jnp.float32)
+    group = TILE // SPAN
+    causal_bias = jnp.concatenate([causal_bias] * group, 0)
+    slot = lax.broadcasted_iota(jnp.int32, (1, PREFIX), 1)
+    slot_bias = jnp.where(slot < len_ref[0], 0.0, MASKED).astype(jnp.float32)
+    score_scale = HD ** (-0.5) * math.log2(math.e)
+
+    table = tables(index_own[...])
+
+    for part in range(2):
+        gather_copy(0, 0, part).wait_recv()
+        gather_copy(0, 2, part).start()
+
+        @pl.when(has_prev)
+        def _():
+            shift_copy(part).wait_recv()
+
+        tokens[1, rows_of(me, part)] = normed(carried_in[part * HALF : (part + 1) * HALF])
+        gather_copy(1, 0, part).start()
+        gather_copy(1, 1, part).start()
+
+    def project(tick):
+        def tile(number, carry):
+            columns = pl.ds(pl.multiple_of(number * TILE, TILE), TILE)
+            projected[:, columns] = jnp.dot(
+                tokens[tick], w_query[:, columns], preferred_element_type=jnp.float32
+            )
+            return carry
+
+        lax.fori_loop(0, query_width // TILE, tile, 0)
+        projected[:, query_width:] = jnp.dot(
+            tokens[tick], w_kv[...], preferred_element_type=jnp.float32
+        )
+
+    def attend(table):
+        for head in range(heads):
+            block = projected[:, head * HD : (head + 1) * HD]
+            queries[head * SPAN : (head + 1) * SPAN] = rotated(block, table)
+        fresh_key = projected[:, query_width : query_width + HD].astype(jnp.bfloat16)
+        keys[PREFIX:] = rotated(fresh_key.astype(jnp.float32), table)
+        values[PREFIX:] = projected[:, query_width + HD :].astype(jnp.bfloat16)
+        transposed = (((1,), (1,)), ((), ()))
+        for block in range(heads // group):
+            query = queries[block * TILE : (block + 1) * TILE]
+            prefix = lax.dot_general(
+                query, keys[:PREFIX], transposed, preferred_element_type=jnp.float32
+            )
+            fresh = lax.dot_general(
+                query, keys[PREFIX:], transposed, preferred_element_type=jnp.float32
+            )
+            prefix = prefix * score_scale + slot_bias
+            fresh = fresh * score_scale + causal_bias
+            peak = jnp.maximum(
+                jnp.max(prefix, axis=-1, keepdims=True), jnp.max(fresh, axis=-1, keepdims=True)
+            )
+            prefix = jnp.exp2(prefix - peak)
+            fresh = jnp.exp2(fresh - peak)
+            total = jnp.sum(prefix, axis=-1, keepdims=True) + jnp.sum(
+                fresh, axis=-1, keepdims=True
+            )
+            mixed = jnp.dot(
+                prefix.astype(jnp.bfloat16), values[:PREFIX], preferred_element_type=jnp.float32
+            ) + jnp.dot(
+                fresh.astype(jnp.bfloat16), values[PREFIX:], preferred_element_type=jnp.float32
+            )
+            mixed = (mixed / total).astype(jnp.bfloat16)
+            for place in range(group):
+                head = block * group + place
+                attended[:, head * HD : (head + 1) * HD] = mixed[place * SPAN : (place + 1) * SPAN]
+
+    def pass_on(tick, number):
+        columns = slice(number * chunk, (number + 1) * chunk)
+        pair_copy(tick, number).wait_recv()
+        far_send[tick, number] = (
+            partial[rows_of(far), columns] + pair_recv[tick, number, 1].astype(jnp.float32)
+        ).astype(jnp.bfloat16)
+        far_copy(tick, number).start()
+        own_sum[tick, :, columns] = partial[rows_of(me), columns] + pair_recv[
+            tick, number, 0
+        ].astype(jnp.float32)
+
+    def emit(tick):
+        for number in range(OUT_CHUNKS):
+            columns = slice(number * chunk, (number + 1) * chunk)
+
+            def tile(step, carry):
+                place = pl.ds(pl.multiple_of(number * chunk + step * TILE, TILE), TILE)
+                partial[:, place] = jnp.dot(
+                    attended[...], w_out[:, place], preferred_element_type=jnp.float32
+                )
+                return carry
+
+            lax.fori_loop(0, chunk // TILE, tile, 0)
+            pair_send[tick, number, 0] = partial[rows_of(pair), columns].astype(jnp.bfloat16)
+            pair_send[tick, number, 1] = partial[rows_of(far_pair), columns].astype(jnp.bfloat16)
+            pair_copy(tick, number).start()
+            if number > 0:
+                pass_on(tick, number - 1)
+        pass_on(tick, OUT_CHUNKS - 1)
+
+    def summed(tick, number):
+        columns = slice(number * chunk, (number + 1) * chunk)
+        far_copy(tick, number).wait_recv()
+        return (own_sum[tick, :, columns] + far_recv[tick, number].astype(jnp.float32)).astype(
+            jnp.bfloat16
+        )
+
+    for part in range(2):
+        for leg in (1, 2):
+            gather_copy(0, leg, part).wait_recv()
+    for load in loads[:5]:
+        load.wait()
+    project(0)
+    for part in range(2):
+        gather_copy(1, 0, part).wait_recv()
+        gather_copy(1, 2, part).start()
+    for load in loads[5:]:
+        load.wait()
+    attend(table)
+    emit(0)
+
+    for part in range(2):
+        for leg in (1, 2):
+            gather_copy(1, leg, part).wait_recv()
+    project(1)
+
+    @pl.when(has_prev)
+    def _():
+        index_copy().wait_recv()
+
+    attend(tables(index_in[...]))
+    for number in range(OUT_CHUNKS):
+        first_out[number] = summed(0, number)
+
+        @pl.when(has_next)
+        def _():
+            out_copy(number).start()
+
+    emit(1)
+    for number in range(OUT_CHUNKS):
+        columns = slice(number * chunk, (number + 1) * chunk)
+
+        @pl.when(has_prev)
+        def _():
+            out_copy(number).wait_recv()
+
+        carried_ref[0, :, columns] = (
+            carried_in[:, columns].astype(jnp.float32) + out_in[number].astype(jnp.float32)
+        ).astype(jnp.bfloat16)
+    for number in range(OUT_CHUNKS):
+        columns = slice(number * chunk, (number + 1) * chunk)
+        output_ref[0, :, columns] = summed(1, number)
+
+    for tick in range(2):
+        for part in range(2):
+            for leg in range(3):
+                gather_copy(tick, leg, part).wait_send()
+        for number in range(OUT_CHUNKS):
+            pair_copy(tick, number).wait_send()
+            far_copy(tick, number).wait_send()
+
+    @pl.when(has_next)
+    def _():
+        for part in range(2):
+            shift_copy(part).wait_send()
+        index_copy().wait_send()
+        for number in range(OUT_CHUNKS):
+            out_copy(number).wait_send()
+
+
+def fused(
+    sections,
+    residual,
+    pending,
+    span_index,
+    prefix_len,
+    norm_gain,
+    w_query,
+    w_kv,
+    w_out,
+    prefix_cache,
+):
+    features, query_width = w_query.shape[1:]
+    pair_width = w_kv.shape[2]
+    chunk = features // OUT_CHUNKS
+    exponents = -np.arange(0, HD, 2, dtype=np.float64) / HD
+    inverse = np.tile((rope_base**exponents).astype(np.float32), 2)
+    inverse = jnp.asarray(np.tile(inverse[None], (8, 1)))
+    smem = pl.BlockSpec(memory_space=pltpu.SMEM)
+    vmem = pl.BlockSpec(memory_space=pltpu.VMEM)
+    whole = pl.BlockSpec(memory_space=pl.ANY)
+    half = jnp.bfloat16
+    dma = pltpu.SemaphoreType.DMA
+    return pl.pallas_call(
+        functools.partial(fused_kernel, sections),
+        out_shape=(
+            jax.ShapeDtypeStruct(residual.shape, half),
+            jax.ShapeDtypeStruct(residual.shape, half),
+        ),
+        in_specs=[smem, smem, vmem, vmem, vmem, vmem, whole, whole, whole, whole],
+        out_specs=(vmem, vmem),
+        scratch_shapes=[
+            pltpu.VMEM((features, query_width), half),
+            pltpu.VMEM((features, pair_width), half),
+            pltpu.VMEM((query_width, features), half),
+            pltpu.VMEM((PREFIX + SPAN, HD), half),
+            pltpu.VMEM((PREFIX + SPAN, HD), half),
+            pltpu.VMEM((2, SPAN, features), half),
+            pltpu.VMEM((ROWS, features), half),
+            pltpu.VMEM((ROWS, features), half),
+            pltpu.VMEM((8, HD), jnp.int32),
+            pltpu.VMEM((8, HD), jnp.int32),
+            pltpu.VMEM((SPAN, query_width + pair_width), jnp.float32),
+            pltpu.VMEM((query_width // HD * SPAN, HD), half),
+            pltpu.VMEM((SPAN, query_width), half),
+            pltpu.VMEM((SPAN, features), jnp.float32),
+            pltpu.VMEM((2, ROWS, features), jnp.float32),
+            pltpu.VMEM((2, OUT_CHUNKS, 2, ROWS, chunk), half),
+            pltpu.VMEM((2, OUT_CHUNKS, 2, ROWS, chunk), half),
+            pltpu.VMEM((2, OUT_CHUNKS, ROWS, chunk), half),
+            pltpu.VMEM((2, OUT_CHUNKS, ROWS, chunk), half),
+            pltpu.VMEM((OUT_CHUNKS, ROWS, chunk), half),
+            pltpu.VMEM((OUT_CHUNKS, ROWS, chunk), half),
+            dma((11,)),
+            dma((2, 3, 2)),
+            dma((2, 3, 2)),
+            dma((3,)),
+            dma((3,)),
+            dma((2, OUT_CHUNKS)),
+            dma((2, OUT_CHUNKS)),
+            dma((2, OUT_CHUNKS)),
+            dma((2, OUT_CHUNKS)),
+            dma((OUT_CHUNKS,)),
+            dma((OUT_CHUNKS,)),
+        ],
+        compiler_params=pltpu.CompilerParams(
+            collective_id=0, has_side_effects=True, vmem_limit_bytes=56 * 1024 * 1024
+        ),
+        name="fused_relay",
+    )(
+        span_index,
+        prefix_len,
+        residual,
+        pending,
+        norm_gain,
+        inverse,
+        w_query,
+        w_kv,
+        w_out,
+        prefix_cache,
+    )
+
+
 def solution(mesh):
     in_specs = (
         P("segment", "tp", None),
@@ -159,4 +624,7 @@
         P("segment", "tp", None),
     )
     out_specs = (P("segment", "tp", None), P("segment", "tp", None))
-    return jax.shard_map(shards, mesh=mesh, in_specs=in_specs, out_specs=out_specs, check_vma=False)
+    body = shards
+    if mesh.shape["tp"] == TP == KV_HEADS and TICKS == 2:
+        body = functools.partial(fused, mesh.shape["segment"])
+    return jax.shard_map(body, mesh=mesh, in_specs=in_specs, out_specs=out_specs, check_vma=False)

time: 145 us -> 48.8 us (0.34)
  waiting for transfers between devices: 56.3 us -> 0 us
  Pallas kernels: 0 us -> 43.3 us
  matrix products: 35.8 us -> 0 us
  between operations: 16 us -> 1.93 us
  other arithmetic: 12.4 us -> 0 us
  starting transfers between devices: 12.4 us -> 0 us
  local copies, waits for them, and re-layouts: 11.6 us -> 3.34 us
    reduce_scatter x2 -> x0, waiting for transfers between devices: 50 us -> none  [shards(): lax.psum_scatter(jnp.dot(attended, weight_out, preferred_element_type=jnp...]
    pallas_call x0 -> x1, Pallas kernels: none -> 43.3 us  [fused(): pl.pallas_call(functools.partial(fused_kernel, sections), out_shape=(jax....]
    dot_general x14 -> x0, matrix products: 35.8 us -> none  [the longest x2 12.5 us: shards(): jnp.dot(block_rows, weight_query, preferred_element_type=jnp.float32)]
    ppermute x3 -> x0, starting transfers between devices: 12.3 us -> none  [shifted(): return lax.ppermute(block, axis, route)]
    dot_general x1 -> x0, local copies, waits for them, and re-layouts: 11.3 us -> none  [shards(): jnp.dot(block_rows, weight_query, preferred_element_type=jnp.float32)]
    all_gather x2 -> x0, waiting for transfers between devices: 5.95 us -> none  [shards(): block_rows = lax.all_gather(normed, 'tp', axis=0, tiled=True)]
    reduce_sum x5 -> x0, other arithmetic: 4.34 us -> none  [the longest x1 2.88 us: shards(): jnp.sum(exp_prefix, axis=-1, keepdims=True)]
    convert_element_type x7 -> x0, other arithmetic: 3.81 us -> none  [the longest x1 1.87 us: shards(): carried = (widths + pending_now.astype(jnp.float32)).astype(jnp.bfloat16)]
  transfers between devices with their start and end apart: 7 -> 0, of which waited for: 4 -> 0; matrix products, arithmetic and copies ran while one was open for 24% -> 0% of each run, Pallas kernels for 0% -> 0%
where the time goes in v1:
time: 48.8 us; the launch traced here: 48.5 us
  Pallas kernels  43.3 us (89%)
  local copies, waits for them, and re-layouts  3.34 us (7%)
  between operations  1.93 us (4%)
    pallas_call x1, Pallas kernels, fused(): pl.pallas_call(functools.partial(fused_kernel, sections), out_shape=(jax....  43.3 us
    unnamed x2, local copies, waits for them, and re-layouts  3.34 us

profile of v1, /device:TPU:0, one launch (start us, length us, event | category | flops | bytes accessed | tf_op | source)
XLA Modules:
  0.0 48.5 jit_solution(17972542194884766483)
XLA Ops:
  1.9 43.3 %fused_relay.1 = (bf16[1,32,4096]{2,1,0:T(8,128)(2,1)}, bf16[1,32,4096]{2,1,0:T(8,128)(2,1)}) custom-call(s32[1]{0:T(128)S(6)} %copy.14.span_ref, s32[1]{0:T(128)S(6)} %copy.15.len_ref, bf16[1,32,4096]{2,1,0:T(8,128)(2,1)} %residual_ref.1, bf16[1,32,4096]{2,1,0:T(8,128)(2,1)} %pending_ref.1, bf16[1,4096]{1,0:T(2,128)(2,1)} %gain_ref.1, ...), custom_call_target="tpu_custom_call" | custom-call | tf_op jit(solution)/shard_map/fused_relay/pallas_call | solution.py:554
  45.2 1.7 %copy.16 = bf16[1,32,4096]{2,1,0:T(8,128)(2,1)} copy(bf16[1,32,4096]{2,1,0:T(8,128)(2,1)} %get-tuple-element.4) | data formatting | bytes 524288
  46.9 1.7 %copy.17 = bf16[1,32,4096]{2,1,0:T(8,128)(2,1)} copy(bf16[1,32,4096]{2,1,0:T(8,128)(2,1)} %get-tuple-element.5) | data formatting | bytes 524288

commit v2 on v1

--- a/solution.py
+++ b/solution.py
@@ -154,9 +154,11 @@
 
 TP = 4
 ROWS = SPAN // TP
-HALF = ROWS // 2
+HALF = 2 * ROWS
+PIECE = ROWS // 2
 OUT_CHUNKS = 4
 TILE = 256
+WIDE = 512
 MASKED = -1e30
 
 
@@ -164,8 +166,8 @@
     sections,
     span_ref,
     len_ref,
-    residual_ref,
-    pending_ref,
+    residual_hbm,
+    pending_hbm,
     gain_ref,
     inverse_ref,
     w_query_hbm,
@@ -174,27 +176,36 @@
     cache_hbm,
     carried_ref,
     output_ref,
+    residual,
+    pending,
     w_query,
     w_kv,
     w_out,
     keys,
     values,
+    span_keys,
+    span_values,
     tokens,
     carried_own,
     carried_in,
     index_own,
     index_in,
+    cosines,
+    sines,
     projected,
     queries,
+    peaks,
+    totals,
+    mixes,
     attended,
     partial,
-    own_sum,
     pair_send,
     pair_recv,
     far_send,
     far_recv,
     first_out,
     out_in,
+    row_sem,
     load_sem,
     gather_send,
     gather_recv,
@@ -213,20 +224,37 @@
     chunk = features // OUT_CHUNKS
     seg = lax.axis_index("segment")
     me = lax.axis_index("tp")
-    pair = me + 1 - 2 * lax.rem(me, 2)
+    core = lax.rem(me, 2)
+    side = me // 2
+    pair = me + 1 - 2 * core
     far = lax.rem(me + 2, TP)
-    far_pair = lax.rem(pair + 2, TP)
     has_prev = seg > 0
     has_next = seg < sections - 1
 
+    barrier = pltpu.get_barrier_semaphore()
+    for partner in (pair, far):
+        pl.semaphore_signal(barrier, inc=1, device_id={"tp": partner})
+
+    @pl.when(has_prev)
+    def _():
+        pl.semaphore_signal(barrier, inc=1, device_id={"segment": seg - 1})
+
+    @pl.when(has_next)
+    def _():
+        pl.semaphore_signal(barrier, inc=1, device_id={"segment": seg + 1})
+
+    row_loads = [
+        pltpu.make_async_copy(residual_hbm.at[0], residual, row_sem.at[0]),
+        pltpu.make_async_copy(pending_hbm.at[0], pending, row_sem.at[1]),
+    ]
     loads = []
     quarter = features // 4
     for part in range(4):
         span = pl.ds(part * quarter, quarter)
         loads.append((w_query_hbm.at[0, span], w_query.at[span]))
     loads.append((w_kv_hbm.at[0], w_kv))
-    loads.append((cache_hbm.at[0, :, pl.ds(0, HD)], keys.at[pl.ds(0, PREFIX)]))
-    loads.append((cache_hbm.at[0, :, pl.ds(HD, HD)], values.at[pl.ds(0, PREFIX)]))
+    loads.append((cache_hbm.at[0, :, pl.ds(0, HD)], keys))
+    loads.append((cache_hbm.at[0, :, pl.ds(HD, HD)], values))
     quarter_out = query_width // 4
     for part in range(4):
         span = pl.ds(part * quarter_out, quarter_out)
@@ -235,27 +263,15 @@
         pltpu.make_async_copy(source, target, load_sem.at[number])
         for number, (source, target) in enumerate(loads)
     ]
-    for load in loads:
+    for load in row_loads + loads:
         load.start()
 
-    barrier = pltpu.get_barrier_semaphore()
-    for partner in (pair, far):
-        pl.semaphore_signal(barrier, inc=1, device_id={"tp": partner})
-
-    @pl.when(has_prev)
-    def _():
-        pl.semaphore_signal(barrier, inc=1, device_id={"segment": seg - 1})
-
-    @pl.when(has_next)
-    def _():
-        pl.semaphore_signal(barrier, inc=1, device_id={"segment": seg + 1})
-
     gain = gain_ref[...].astype(jnp.float32)
 
-    def rows_of(rank, part=None):
+    def rows_of(slot, which, part=None):
         if part is None:
-            return pl.ds(pl.multiple_of(rank * ROWS, ROWS), ROWS)
-        return pl.ds(pl.multiple_of(rank * ROWS + part * HALF, HALF), HALF)
+            return pl.ds(pl.multiple_of(slot * HALF + which * ROWS, ROWS), ROWS)
+        return pl.ds(pl.multiple_of(slot * HALF + which * ROWS + part * PIECE, PIECE), PIECE)
 
     def normed(rows):
         widths = rows.astype(jnp.float32)
@@ -263,18 +279,17 @@
         return (widths * lax.rsqrt(mean_square + norm_eps) * gain).astype(jnp.bfloat16)
 
     def gather_copy(tick, leg, part):
-        rank = far if leg == 2 else me
-        block = tokens.at[tick, rows_of(rank, part)]
+        here, there = ((0, 1), (0, 0), (1, 1))[leg]
         return pltpu.make_async_remote_copy(
-            src_ref=block,
-            dst_ref=block,
+            src_ref=tokens.at[rows_of(2 * tick + here, core, part)],
+            dst_ref=tokens.at[rows_of(2 * tick + there, core, part)],
             send_sem=gather_send.at[tick, leg, part],
             recv_sem=gather_recv.at[tick, leg, part],
             device_id={"tp": far if leg == 0 else pair},
         )
 
     def shift_copy(part):
-        rows = pl.ds(part * HALF, HALF)
+        rows = pl.ds(part * PIECE, PIECE)
         return pltpu.make_async_remote_copy(
             src_ref=carried_own.at[rows],
             dst_ref=carried_in.at[rows],
@@ -292,12 +307,12 @@
             device_id={"segment": seg + 1},
         )
 
-    def pair_copy(tick, number):
+    def pair_copy(tick, number, kind):
         return pltpu.make_async_remote_copy(
-            src_ref=pair_send.at[tick, number],
-            dst_ref=pair_recv.at[tick, number],
-            send_sem=pair_send_sem.at[tick, number],
-            recv_sem=pair_recv_sem.at[tick, number],
+            src_ref=pair_send.at[tick, number, kind],
+            dst_ref=pair_recv.at[tick, number, kind],
+            send_sem=pair_send_sem.at[tick, number, kind],
+            recv_sem=pair_recv_sem.at[tick, number, kind],
             device_id={"tp": pair},
         )
 
@@ -319,9 +334,11 @@
             device_id={"segment": seg + 1},
         )
 
-    tokens[0, rows_of(me)] = normed(residual_ref[0])
+    row_loads[0].wait()
+    tokens[rows_of(0, core)] = normed(residual[...])
+    row_loads[1].wait()
     carried_own[...] = (
-        residual_ref[0].astype(jnp.float32) + pending_ref[0].astype(jnp.float32)
+        residual[...].astype(jnp.float32) + pending[...].astype(jnp.float32)
     ).astype(jnp.bfloat16)
     index_own[...] = jnp.full(index_own.shape, span_ref[0], jnp.int32)
 
@@ -346,28 +363,30 @@
         out_in[...] = jnp.zeros_like(out_in)
 
     lane = lax.broadcasted_iota(jnp.int32, (SPAN, HD), 1)
-    row = lax.broadcasted_iota(jnp.int32, (SPAN, HD), 0)
-
-    def tables(index_tile):
-        positions = (index_tile[0:1, :] * SPAN + row).astype(jnp.float32)
+    token = (lax.broadcasted_iota(jnp.int32, (SPAN, HD), 0) + side * HALF) & (SPAN - 1)
+    key_token = (lane + side * HALF) & (SPAN - 1)
+
+    def tables(tick, index_tile):
+        positions = (index_tile[0:1, :] * SPAN + token).astype(jnp.float32)
         angles = positions * inverse_ref[0:1, :]
         sine = jnp.sin(angles)
-        return jnp.cos(angles), jnp.where(lane < HD // 2, -sine, sine)
-
-    def rotated(block, table):
-        cosine, sine = table
-        return (block * cosine + pltpu.roll(block, HD // 2, 1) * sine).astype(jnp.bfloat16)
-
-    causal_bias = jnp.where(lane <= row, 0.0, MASKED).astype(jnp.float32)
-    group = TILE // SPAN
-    causal_bias = jnp.concatenate([causal_bias] * group, 0)
-    slot = lax.broadcasted_iota(jnp.int32, (1, PREFIX), 1)
-    slot_bias = jnp.where(slot < len_ref[0], 0.0, MASKED).astype(jnp.float32)
+        cosines[tick] = jnp.cos(angles)
+        sines[tick] = jnp.where(lane < HD // 2, -sine, sine)
+
+    def rotated(block, slot):
+        tick, half = slot // 2, slot % 2
+        rows = slice(half * HALF, (half + 1) * HALF)
+        turned = pltpu.roll(block, HD // 2, 1)
+        return (block * cosines[tick, rows] + turned * sines[tick, rows]).astype(jnp.bfloat16)
+
+    causal_bias = jnp.where(key_token <= token, 0.0, MASKED).astype(jnp.float32)
+    group = TILE // HALF
+    slot_index = lax.broadcasted_iota(jnp.int32, (1, PREFIX), 1)
+    slot_bias = jnp.where(slot_index < len_ref[0], 0.0, MASKED).astype(jnp.float32)
     score_scale = HD ** (-0.5) * math.log2(math.e)
-
-    table = tables(index_own[...])
-
-    for part in range(2):
+    transposed = (((1,), (1,)), ((), ()))
+
+    def relay_and_shift(part):
         gather_copy(0, 0, part).wait_recv()
         gather_copy(0, 2, part).start()
 
@@ -375,128 +394,167 @@
         def _():
             shift_copy(part).wait_recv()
 
-        tokens[1, rows_of(me, part)] = normed(carried_in[part * HALF : (part + 1) * HALF])
+        rows = carried_in[part * PIECE : (part + 1) * PIECE]
+        tokens[rows_of(2, core, part)] = normed(rows)
         gather_copy(1, 0, part).start()
         gather_copy(1, 1, part).start()
 
-    def project(tick):
+    def project(slots):
+        first, count = slots[0] * HALF, len(slots) * HALF
+
         def tile(number, carry):
-            columns = pl.ds(pl.multiple_of(number * TILE, TILE), TILE)
-            projected[:, columns] = jnp.dot(
-                tokens[tick], w_query[:, columns], preferred_element_type=jnp.float32
+            columns = pl.ds(pl.multiple_of(number * WIDE, WIDE), WIDE)
+            projected[:count, columns] = jnp.dot(
+                tokens[first : first + count], w_query[:, columns], preferred_element_type=jnp.float32
             )
             return carry
 
-        lax.fori_loop(0, query_width // TILE, tile, 0)
-        projected[:, query_width:] = jnp.dot(
-            tokens[tick], w_kv[...], preferred_element_type=jnp.float32
-        )
-
-    def attend(table):
-        for head in range(heads):
-            block = projected[:, head * HD : (head + 1) * HD]
-            queries[head * SPAN : (head + 1) * SPAN] = rotated(block, table)
-        fresh_key = projected[:, query_width : query_width + HD].astype(jnp.bfloat16)
-        keys[PREFIX:] = rotated(fresh_key.astype(jnp.float32), table)
-        values[PREFIX:] = projected[:, query_width + HD :].astype(jnp.bfloat16)
-        transposed = (((1,), (1,)), ((), ()))
+        lax.fori_loop(0, query_width // WIDE, tile, 0)
+        projected[:count, query_width:] = jnp.dot(
+            tokens[first : first + count], w_kv[...], preferred_element_type=jnp.float32
+        )
+
+    def spread(slots):
+        for place, slot in enumerate(slots):
+            rows = slice(place * HALF, (place + 1) * HALF)
+            for head in range(heads):
+                block = projected[rows, head * HD : (head + 1) * HD]
+                queries[slot, head * HALF : (head + 1) * HALF] = rotated(block, slot)
+            tick, half = slot // 2, slot % 2
+            span = slice(half * HALF, (half + 1) * HALF)
+            fresh = projected[rows, query_width : query_width + HD].astype(jnp.bfloat16)
+            span_keys[tick, span] = rotated(fresh.astype(jnp.float32), slot)
+            span_values[tick, span] = projected[rows, query_width + HD :].astype(jnp.bfloat16)
+
+    def attend_prefix(slot):
+        half = slot % 2
         for block in range(heads // group):
-            query = queries[block * TILE : (block + 1) * TILE]
-            prefix = lax.dot_general(
-                query, keys[:PREFIX], transposed, preferred_element_type=jnp.float32
+            rows = slice(block * TILE, (block + 1) * TILE)
+            scores = lax.dot_general(
+                queries[slot, rows], keys[...], transposed, preferred_element_type=jnp.float32
             )
-            fresh = lax.dot_general(
-                query, keys[PREFIX:], transposed, preferred_element_type=jnp.float32
+            scores = scores * score_scale + slot_bias
+            peak = jnp.max(scores, axis=-1, keepdims=True)
+            weights = jnp.exp2(scores - peak)
+            total = jnp.sum(weights, axis=-1, keepdims=True)
+            mixes[half, rows] = jnp.dot(
+                weights.astype(jnp.bfloat16), values[...], preferred_element_type=jnp.float32
             )
-            prefix = prefix * score_scale + slot_bias
-            fresh = fresh * score_scale + causal_bias
-            peak = jnp.maximum(
-                jnp.max(prefix, axis=-1, keepdims=True), jnp.max(fresh, axis=-1, keepdims=True)
+            peaks[half, rows] = jnp.broadcast_to(peak, (TILE, HD))
+            totals[half, rows] = jnp.broadcast_to(total, (TILE, HD))
+
+    def attend_span(slot):
+        tick, half = slot // 2, slot % 2
+        bias = causal_bias[half * HALF : (half + 1) * HALF]
+        bias = jnp.concatenate([bias] * group, 0)
+        for block in range(heads // group):
+            rows = slice(block * TILE, (block + 1) * TILE)
+            scores = lax.dot_general(
+                queries[slot, rows], span_keys[tick], transposed, preferred_element_type=jnp.float32
             )
-            prefix = jnp.exp2(prefix - peak)
-            fresh = jnp.exp2(fresh - peak)
-            total = jnp.sum(prefix, axis=-1, keepdims=True) + jnp.sum(
-                fresh, axis=-1, keepdims=True
-            )
-            mixed = jnp.dot(
-                prefix.astype(jnp.bfloat16), values[:PREFIX], preferred_element_type=jnp.float32
-            ) + jnp.dot(
-                fresh.astype(jnp.bfloat16), values[PREFIX:], preferred_element_type=jnp.float32
+            scores = scores * score_scale + bias
+            before = peaks[half, rows]
+            peak = jnp.maximum(before, jnp.max(scores, axis=-1, keepdims=True))
+            weights = jnp.exp2(scores - peak)
+            shrink = jnp.exp2(before - peak)
+            total = totals[half, rows] * shrink + jnp.sum(weights, axis=-1, keepdims=True)
+            mixed = mixes[half, rows] * shrink + jnp.dot(
+                weights.astype(jnp.bfloat16), span_values[tick], preferred_element_type=jnp.float32
             )
             mixed = (mixed / total).astype(jnp.bfloat16)
             for place in range(group):
                 head = block * group + place
-                attended[:, head * HD : (head + 1) * HD] = mixed[place * SPAN : (place + 1) * SPAN]
+                attended[half * HALF : (half + 1) * HALF, head * HD : (head + 1) * HD] = mixed[
+                    place * HALF : (place + 1) * HALF
+                ]
 
     def pass_on(tick, number):
         columns = slice(number * chunk, (number + 1) * chunk)
-        pair_copy(tick, number).wait_recv()
+        pair_copy(tick, number, 1).wait_recv()
         far_send[tick, number] = (
-            partial[rows_of(far), columns] + pair_recv[tick, number, 1].astype(jnp.float32)
+            partial[rows_of(1, core), columns] + pair_recv[tick, number, 1].astype(jnp.float32)
         ).astype(jnp.bfloat16)
         far_copy(tick, number).start()
-        own_sum[tick, :, columns] = partial[rows_of(me), columns] + pair_recv[
-            tick, number, 0
-        ].astype(jnp.float32)
-
-    def emit(tick):
+
+    def emit(tick, halves):
+        first, last = halves[0] * HALF, (halves[-1] + 1) * HALF
         for number in range(OUT_CHUNKS):
             columns = slice(number * chunk, (number + 1) * chunk)
-
-            def tile(step, carry):
-                place = pl.ds(pl.multiple_of(number * chunk + step * TILE, TILE), TILE)
-                partial[:, place] = jnp.dot(
-                    attended[...], w_out[:, place], preferred_element_type=jnp.float32
+            partial[first:last, columns] = jnp.dot(
+                attended[first:last], w_out[:, columns], preferred_element_type=jnp.float32
+            )
+            for kind in reversed(halves):
+                pair_send[tick, number, kind] = partial[rows_of(kind, 1 - core), columns].astype(
+                    jnp.bfloat16
                 )
-                return carry
-
-            lax.fori_loop(0, chunk // TILE, tile, 0)
-            pair_send[tick, number, 0] = partial[rows_of(pair), columns].astype(jnp.bfloat16)
-            pair_send[tick, number, 1] = partial[rows_of(far_pair), columns].astype(jnp.bfloat16)
-            pair_copy(tick, number).start()
-            if number > 0:
+                pair_copy(tick, number, kind).start()
+            if 1 in halves and number > 0:
                 pass_on(tick, number - 1)
-        pass_on(tick, OUT_CHUNKS - 1)
+        if 1 in halves:
+            pass_on(tick, OUT_CHUNKS - 1)
 
     def summed(tick, number):
         columns = slice(number * chunk, (number + 1) * chunk)
+        pair_copy(tick, number, 0).wait_recv()
+        beside = partial[rows_of(0, core), columns] + pair_recv[tick, number, 0].astype(jnp.float32)
         far_copy(tick, number).wait_recv()
-        return (own_sum[tick, :, columns] + far_recv[tick, number].astype(jnp.float32)).astype(
-            jnp.bfloat16
-        )
-
+        return (beside + far_recv[tick, number].astype(jnp.float32)).astype(jnp.bfloat16)
+
+    def finish_first(number):
+        first_out[number] = summed(0, number)
+
+        @pl.when(has_next)
+        def _():
+            out_copy(number).start()
+
+    tables(0, index_own[...])
     for part in range(2):
-        for leg in (1, 2):
-            gather_copy(0, leg, part).wait_recv()
+        gather_copy(0, 1, part).wait_recv()
     for load in loads[:5]:
         load.wait()
-    project(0)
+    project((0,))
+    relay_and_shift(0)
+    spread((0,))
+    for load in loads[5:7]:
+        load.wait()
+    attend_prefix(0)
+    relay_and_shift(1)
+
+    @pl.when(has_prev)
+    def _():
+        index_copy().wait_recv()
+
+    tables(1, index_in[...])
+    for part in range(2):
+        gather_copy(0, 2, part).wait_recv()
+        gather_copy(1, 1, part).wait_recv()
+    project((1, 2))
+    spread((1, 2))
+    attend_prefix(1)
+    attend_span(1)
+    attend_span(0)
+    for load in loads[7:]:
+        load.wait()
     for part in range(2):
         gather_copy(1, 0, part).wait_recv()
         gather_copy(1, 2, part).start()
-    for load in loads[5:]:
-        load.wait()
-    attend(table)
-    emit(0)
+    emit(0, (0, 1))
 
     for part in range(2):
-        for leg in (1, 2):
-            gather_copy(1, leg, part).wait_recv()
-    project(1)
-
-    @pl.when(has_prev)
-    def _():
-        index_copy().wait_recv()
-
-    attend(tables(index_in[...]))
+        gather_copy(1, 2, part).wait_recv()
+    project((3,))
+    spread((3,))
+    attend_prefix(3)
+    attend_span(3)
+    emit(1, (1,))
     for number in range(OUT_CHUNKS):
-        first_out[number] = summed(0, number)
-
-        @pl.when(has_next)
-        def _():
-            out_copy(number).start()
-
-    emit(1)
+        finish_first(number)
+    attend_prefix(2)
+    attend_span(2)
+    emit(1, (0,))
+    for number in range(OUT_CHUNKS):
+        columns = slice(number * chunk, (number + 1) * chunk)
+        output_ref[0, :, columns] = summed(1, number)
     for number in range(OUT_CHUNKS):
         columns = slice(number * chunk, (number + 1) * chunk)
 
@@ -507,16 +565,14 @@
         carried_ref[0, :, columns] = (
             carried_in[:, columns].astype(jnp.float32) + out_in[number].astype(jnp.float32)
         ).astype(jnp.bfloat16)
-    for number in range(OUT_CHUNKS):
-        columns = slice(number * chunk, (number + 1) * chunk)
-        output_ref[0, :, columns] = summed(1, number)
 
     for tick in range(2):
         for part in range(2):
             for leg in range(3):
                 gather_copy(tick, leg, part).wait_send()
         for number in range(OUT_CHUNKS):
-            pair_copy(tick, number).wait_send()
+            for kind in range(2):
+                pair_copy(tick, number, kind).wait_send()
             far_copy(tick, number).wait_send()
 
     @pl.when(has_next)
@@ -526,6 +582,39 @@
         index_copy().wait_send()
         for number in range(OUT_CHUNKS):
             out_copy(number).wait_send()
+
+
+def hand_out_kernel(carried_from, output_from, carried_to, output_to, sem):
+    rows = carried_from.shape[1] // 2
+    copies = [
+        pltpu.make_async_copy(
+            source.at[0, pl.ds(part * rows, rows)],
+            target.at[0, pl.ds(part * rows, rows)],
+            sem.at[place, part],
+        )
+        for place, (source, target) in enumerate(
+            ((carried_from, carried_to), (output_from, output_to))
+        )
+        for part in range(2)
+    ]
+    for copy in copies:
+        copy.start()
+    for copy in copies:
+        copy.wait()
+
+
+def hand_out(carried, output):
+    whole = pl.BlockSpec(memory_space=pl.ANY)
+    shape = jax.ShapeDtypeStruct(carried.shape, carried.dtype)
+    return pl.pallas_call(
+        hand_out_kernel,
+        out_shape=(shape, shape),
+        in_specs=[whole, whole],
+        out_specs=(whole, whole),
+        scratch_shapes=[pltpu.SemaphoreType.DMA((2, 2))],
+        compiler_params=pltpu.CompilerParams(vmem_limit_bytes=1024 * 1024),
+        name="hand_out",
+    )(carried, output)
 
 
 def fused(
@@ -551,50 +640,59 @@
     whole = pl.BlockSpec(memory_space=pl.ANY)
     half = jnp.bfloat16
     dma = pltpu.SemaphoreType.DMA
-    return pl.pallas_call(
+    carried, output = pl.pallas_call(
         functools.partial(fused_kernel, sections),
         out_shape=(
             jax.ShapeDtypeStruct(residual.shape, half),
             jax.ShapeDtypeStruct(residual.shape, half),
         ),
-        in_specs=[smem, smem, vmem, vmem, vmem, vmem, whole, whole, whole, whole],
+        in_specs=[smem, smem, whole, whole, vmem, vmem, whole, whole, whole, whole],
         out_specs=(vmem, vmem),
         scratch_shapes=[
+            pltpu.VMEM((ROWS, features), half),
+            pltpu.VMEM((ROWS, features), half),
             pltpu.VMEM((features, query_width), half),
             pltpu.VMEM((features, pair_width), half),
             pltpu.VMEM((query_width, features), half),
-            pltpu.VMEM((PREFIX + SPAN, HD), half),
-            pltpu.VMEM((PREFIX + SPAN, HD), half),
-            pltpu.VMEM((2, SPAN, features), half),
+            pltpu.VMEM((PREFIX, HD), half),
+            pltpu.VMEM((PREFIX, HD), half),
+            pltpu.VMEM((2, SPAN, HD), half),
+            pltpu.VMEM((2, SPAN, HD), half),
+            pltpu.VMEM((2 * SPAN, features), half),
             pltpu.VMEM((ROWS, features), half),
             pltpu.VMEM((ROWS, features), half),
             pltpu.VMEM((8, HD), jnp.int32),
             pltpu.VMEM((8, HD), jnp.int32),
+            pltpu.VMEM((2, SPAN, HD), jnp.float32),
+            pltpu.VMEM((2, SPAN, HD), jnp.float32),
             pltpu.VMEM((SPAN, query_width + pair_width), jnp.float32),
-            pltpu.VMEM((query_width // HD * SPAN, HD), half),
+            pltpu.VMEM((4, query_width // HD * HALF, HD), half),
+            pltpu.VMEM((2, query_width // HD * HALF, HD), jnp.float32),
+            pltpu.VMEM((2, query_width // HD * HALF, HD), jnp.float32),
+            pltpu.VMEM((2, query_width // HD * HALF, HD), jnp.float32),
             pltpu.VMEM((SPAN, query_width), half),
             pltpu.VMEM((SPAN, features), jnp.float32),
-            pltpu.VMEM((2, ROWS, features), jnp.float32),
             pltpu.VMEM((2, OUT_CHUNKS, 2, ROWS, chunk), half),
             pltpu.VMEM((2, OUT_CHUNKS, 2, ROWS, chunk), half),
             pltpu.VMEM((2, OUT_CHUNKS, ROWS, chunk), half),
             pltpu.VMEM((2, OUT_CHUNKS, ROWS, chunk), half),
             pltpu.VMEM((OUT_CHUNKS, ROWS, chunk), half),
             pltpu.VMEM((OUT_CHUNKS, ROWS, chunk), half),
+            dma((2,)),
             dma((11,)),
             dma((2, 3, 2)),
             dma((2, 3, 2)),
             dma((3,)),
             dma((3,)),
-            dma((2, OUT_CHUNKS)),
-            dma((2, OUT_CHUNKS)),
+            dma((2, OUT_CHUNKS, 2)),
+            dma((2, OUT_CHUNKS, 2)),
             dma((2, OUT_CHUNKS)),
             dma((2, OUT_CHUNKS)),
             dma((OUT_CHUNKS,)),
             dma((OUT_CHUNKS,)),
         ],
         compiler_params=pltpu.CompilerParams(
-            collective_id=0, has_side_effects=True, vmem_limit_bytes=56 * 1024 * 1024
+            collective_id=0, has_side_effects=True, vmem_limit_bytes=46 * 1024 * 1024
         ),
         name="fused_relay",
     )(
@@ -609,6 +707,7 @@
         w_out,
         prefix_cache,
     )
+    return hand_out(carried, output)
 
 
 def solution(mesh):

time: 48.8 us -> 44.1 us (0.904); the launches traced: 48.5 us -> 43.2 us
  Pallas kernels: 43.3 us -> 35.1 us
  local copies, waits for them, and re-layouts: 3.34 us -> 6.02 us
    pallas_call x1, Pallas kernels: 43.3 us -> 34.3 us  [fused(): pl.pallas_call(functools.partial(fused_kernel, sections), out_shape=(jax....]
    unnamed x2 -> x12, local copies, waits for them, and re-layouts: 3.34 us -> 6.02 us
    pallas_call x0 -> x1, Pallas kernels: none -> 0.82 us  [hand_out(): pl.pallas_call(hand_out_kernel, out_shape=(shape, shape), in_specs=[whole...]
where the time goes in v2:
time: 44.1 us; the launch traced here: 43.2 us
  Pallas kernels  35.1 us (80%)
  local copies, waits for them, and re-layouts  6.02 us (14%)
  between operations  2.11 us (5%)
    pallas_call x1, Pallas kernels, fused(): pl.pallas_call(functools.partial(fused_kernel, sections), out_shape=(jax....  34.3 us
    unnamed x12, local copies, waits for them, and re-layouts  6.02 us

profile of v2, /device:TPU:0, one launch (start us, length us, event | category | flops | bytes accessed | tf_op | source)
XLA Modules:
  0.0 43.2 jit_solution(1324695113082810318)
XLA Ops:
  1.9 0.0 copy-start
  1.9 1.6 %copy-done = bf16[1,4096,256]{2,1,0:T(8,128)(2,1)S(1)} copy-done((bf16[1,4096,256]{2,1,0:T(8,128)(2,1)S(1)}, bf16[1,4096,256]{2,1,0:T(8,128)(2,1)}, u32[]{:S(2)}) %copy-start) | copy-done | bytes 2097176
  3.5 0.0 copy-start.1
  3.5 1.1 %copy-done.1 = bf16[1,1536,256]{2,1,0:T(8,128)(2,1)S(1)} copy-done((bf16[1,1536,256]{2,1,0:T(8,128)(2,1)S(1)}, bf16[1,1536,256]{2,1,0:T(8,128)(2,1)}, u32[]{:S(2)}) %copy-start.1) | copy-done | bytes 786456
  4.6 0.0 copy-start.2
  4.7 0.9 %copy-done.2 = bf16[1,32,4096]{2,1,0:T(8,128)(2,1)S(1)} copy-done((bf16[1,32,4096]{2,1,0:T(8,128)(2,1)S(1)}, bf16[1,32,4096]{2,1,0:T(8,128)(2,1)}, u32[]{:S(2)}) %copy-start.2) | copy-done | bytes 262168
  5.6 0.0 copy-start.3
  5.6 0.9 %copy-done.3 = bf16[1,32,4096]{2,1,0:T(8,128)(2,1)S(1)} copy-done((bf16[1,32,4096]{2,1,0:T(8,128)(2,1)S(1)}, bf16[1,32,4096]{2,1,0:T(8,128)(2,1)}, u32[]{:S(2)}) %copy-start.3) | copy-done | bytes 262168
  6.5 0.0 copy-start.4
  6.6 0.7 %copy-done.4 = bf16[1,4096]{1,0:T(2,128)(2,1)S(1)} copy-done((bf16[1,4096]{1,0:T(2,128)(2,1)S(1)}, bf16[1,4096]{1,0:T(2,128)(2,1)}, u32[]{:S(2)}) %copy-start.4) | copy-done | bytes 8216
  7.3 0.0 copy-start.5
  7.3 0.7 %copy-done.5 = f32[8,128]{1,0:T(8,128)S(1)} copy-done((f32[8,128]{1,0:T(8,128)S(1)}, f32[8,128]{1,0:T(8,128)}, u32[]{:S(2)}) %copy-start.5) | copy-done | bytes 4120
  8.0 34.3 %fused_relay.1 = (bf16[1,32,4096]{2,1,0:T(8,128)(2,1)S(1)}, bf16[1,32,4096]{2,1,0:T(8,128)(2,1)S(1)}) custom-call(s32[1]{0:T(128)S(6)} %copy.12.span_ref, s32[1]{0:T(128)S(6)} %copy.13.len_ref, bf16[1,32,4096]{2,1,0:T(8,128)(2,1)S(1)} %copy-done.2, bf16[1,32,4096]{2,1,0:T(8,128)(2,1)S(1)} %copy-done.3, bf16[1,4096]{1,0:T(2,128)(2,1)S(1)} %copy-done.4, ...), custom_call_target="tpu_custom_call" | custom-call | tf_op jit(solution)/shard_map/fused_relay/pallas_call | solution.py:643
  42.2 0.8 %hand_out.1 = (bf16[1,32,4096]{2,1,0:T(8,128)(2,1)}, bf16[1,32,4096]{2,1,0:T(8,128)(2,1)}) custom-call(bf16[1,32,4096]{2,1,0:T(8,128)(2,1)S(1)} %get-tuple-element.4.carried_from, bf16[1,32,4096]{2,1,0:T(8,128)(2,1)S(1)} %get-tuple-element.5.output_from), custom_call_target="tpu_custom_call" | custom-call | tf_op jit(solution)/shard_map/hand_out/pallas_call | solution.py:609
Async XLA Ops:
  1.9 1.6 %copy-start = (bf16[1,4096,256]{2,1,0:T(8,128)(2,1)S(1)}, bf16[1,4096,256]{2,1,0:T(8,128)(2,1)}, u32[]{:S(2)}) copy-start(bf16[1,4096,256]{2,1,0:T(8,128)(2,1)} %w_kv_hbm.1) | copy-start | bytes 6291460
  3.5 1.1 %copy-start.1 = (bf16[1,1536,256]{2,1,0:T(8,128)(2,1)S(1)}, bf16[1,1536,256]{2,1,0:T(8,128)(2,1)}, u32[]{:S(2)}) copy-start(bf16[1,1536,256]{2,1,0:T(8,128)(2,1)} %cache_hbm.1) | copy-start | bytes 2359300
  4.6 0.9 %copy-start.2 = (bf16[1,32,4096]{2,1,0:T(8,128)(2,1)S(1)}, bf16[1,32,4096]{2,1,0:T(8,128)(2,1)}, u32[]{:S(2)}) copy-start(bf16[1,32,4096]{2,1,0:T(8,128)(2,1)} %residual_hbm.1) | copy-start | bytes 786436
  5.6 0.9 %copy-start.3 = (bf16[1,32,4096]{2,1,0:T(8,128)(2,1)S(1)}, bf16[1,32,4096]{2,1,0:T(8,128)(2,1)}, u32[]{:S(2)}) copy-start(bf16[1,32,4096]{2,1,0:T(8,128)(2,1)} %pending_hbm.1) | copy-start | bytes 786436
  6.5 0.7 %copy-start.4 = (bf16[1,4096]{1,0:T(2,128)(2,1)S(1)}, bf16[1,4096]{1,0:T(2,128)(2,1)}, u32[]{:S(2)}) copy-start(bf16[1,4096]{1,0:T(2,128)(2,1)} %gain_ref.1) | copy-start | bytes 24580
  7.3 0.7 %copy-start.5 = (f32[8,128]{1,0:T(8,128)S(1)}, f32[8,128]{1,0:T(8,128)}, u32[]{:S(2)}) copy-start(f32[8,128]{1,0:T(8,128)} %constant.2.clone.inverse_ref) | copy-start | bytes 12292

commit v3 on v2

--- a/solution.py
+++ b/solution.py
@@ -168,8 +168,8 @@
     len_ref,
     residual_hbm,
     pending_hbm,
-    gain_ref,
-    inverse_ref,
+    gain_hbm,
+    inverse_hbm,
     w_query_hbm,
     w_kv_hbm,
     w_out_hbm,
@@ -178,6 +178,8 @@
     output_ref,
     residual,
     pending,
+    gain_ref,
+    inverse_ref,
     w_query,
     w_kv,
     w_out,
@@ -195,7 +197,6 @@
     projected,
     queries,
     peaks,
-    totals,
     mixes,
     attended,
     partial,
@@ -245,7 +246,9 @@
 
     row_loads = [
         pltpu.make_async_copy(residual_hbm.at[0], residual, row_sem.at[0]),
+        pltpu.make_async_copy(gain_hbm, gain_ref, row_sem.at[2]),
         pltpu.make_async_copy(pending_hbm.at[0], pending, row_sem.at[1]),
+        pltpu.make_async_copy(inverse_hbm, inverse_ref, row_sem.at[3]),
     ]
     loads = []
     quarter = features // 4
@@ -254,7 +257,7 @@
         loads.append((w_query_hbm.at[0, span], w_query.at[span]))
     loads.append((w_kv_hbm.at[0], w_kv))
     loads.append((cache_hbm.at[0, :, pl.ds(0, HD)], keys))
-    loads.append((cache_hbm.at[0, :, pl.ds(HD, HD)], values))
+    loads.append((cache_hbm.at[0, :, pl.ds(HD, HD)], values.at[:, pl.ds(0, HD)]))
     quarter_out = query_width // 4
     for part in range(4):
         span = pl.ds(part * quarter_out, quarter_out)
@@ -266,8 +269,6 @@
     for load in row_loads + loads:
         load.start()
 
-    gain = gain_ref[...].astype(jnp.float32)
-
     def rows_of(slot, which, part=None):
         if part is None:
             return pl.ds(pl.multiple_of(slot * HALF + which * ROWS, ROWS), ROWS)
@@ -275,6 +276,7 @@
 
     def normed(rows):
         widths = rows.astype(jnp.float32)
+        gain = gain_ref[...].astype(jnp.float32)
         mean_square = jnp.mean(widths * widths, axis=-1, keepdims=True)
         return (widths * lax.rsqrt(mean_square + norm_eps) * gain).astype(jnp.bfloat16)
 
@@ -335,8 +337,9 @@
         )
 
     row_loads[0].wait()
+    row_loads[1].wait()
     tokens[rows_of(0, core)] = normed(residual[...])
-    row_loads[1].wait()
+    row_loads[2].wait()
     carried_own[...] = (
         residual[...].astype(jnp.float32) + pending[...].astype(jnp.float32)
     ).astype(jnp.bfloat16)
@@ -424,7 +427,7 @@
             span = slice(half * HALF, (half + 1) * HALF)
             fresh = projected[rows, query_width : query_width + HD].astype(jnp.bfloat16)
             span_keys[tick, span] = rotated(fresh.astype(jnp.float32), slot)
-            span_values[tick, span] = projected[rows, query_width + HD :].astype(jnp.bfloat16)
+            span_values[tick, span, :HD] = projected[rows, query_width + HD :].astype(jnp.bfloat16)
 
     def attend_prefix(slot):
         half = slot % 2
@@ -436,12 +439,10 @@
             scores = scores * score_scale + slot_bias
             peak = jnp.max(scores, axis=-1, keepdims=True)
             weights = jnp.exp2(scores - peak)
-            total = jnp.sum(weights, axis=-1, keepdims=True)
             mixes[half, rows] = jnp.dot(
                 weights.astype(jnp.bfloat16), values[...], preferred_element_type=jnp.float32
             )
             peaks[half, rows] = jnp.broadcast_to(peak, (TILE, HD))
-            totals[half, rows] = jnp.broadcast_to(total, (TILE, HD))
 
     def attend_span(slot):
         tick, half = slot // 2, slot % 2
@@ -457,10 +458,11 @@
             peak = jnp.maximum(before, jnp.max(scores, axis=-1, keepdims=True))
             weights = jnp.exp2(scores - peak)
             shrink = jnp.exp2(before - peak)
-            total = totals[half, rows] * shrink + jnp.sum(weights, axis=-1, keepdims=True)
-            mixed = mixes[half, rows] * shrink + jnp.dot(
+            fresh = jnp.dot(
                 weights.astype(jnp.bfloat16), span_values[tick], preferred_element_type=jnp.float32
             )
+            total = mixes[half, rows, HD:] * shrink + fresh[:, HD:]
+            mixed = mixes[half, rows, :HD] * shrink + fresh[:, :HD]
             mixed = (mixed / total).astype(jnp.bfloat16)
             for place in range(group):
                 head = block * group + place
@@ -488,10 +490,9 @@
                     jnp.bfloat16
                 )
                 pair_copy(tick, number, kind).start()
-            if 1 in halves and number > 0:
-                pass_on(tick, number - 1)
         if 1 in halves:
-            pass_on(tick, OUT_CHUNKS - 1)
+            for number in range(OUT_CHUNKS):
+                pass_on(tick, number)
 
     def summed(tick, number):
         columns = slice(number * chunk, (number + 1) * chunk)
@@ -507,7 +508,10 @@
         def _():
             out_copy(number).start()
 
+    row_loads[3].wait()
     tables(0, index_own[...])
+    values[:, HD:] = jnp.ones_like(values[:, HD:])
+    span_values[:, :, HD:] = jnp.ones_like(span_values[:, :, HD:])
     for part in range(2):
         gather_copy(0, 1, part).wait_recv()
     for load in loads[:5]:
@@ -545,9 +549,11 @@
     project((3,))
     spread((3,))
     attend_prefix(3)
+    for number in range(OUT_CHUNKS // 2):
+        finish_first(number)
     attend_span(3)
     emit(1, (1,))
-    for number in range(OUT_CHUNKS):
+    for number in range(OUT_CHUNKS // 2, OUT_CHUNKS):
         finish_first(number)
     attend_prefix(2)
     attend_span(2)
@@ -612,7 +618,7 @@
         in_specs=[whole, whole],
         out_specs=(whole, whole),
         scratch_shapes=[pltpu.SemaphoreType.DMA((2, 2))],
-        compiler_params=pltpu.CompilerParams(vmem_limit_bytes=1024 * 1024),
+        compiler_params=pltpu.CompilerParams(vmem_limit_bytes=60 * 1024 * 1024),
         name="hand_out",
     )(carried, output)
 
@@ -637,7 +643,7 @@
     inverse = jnp.asarray(np.tile(inverse[None], (8, 1)))
     smem = pl.BlockSpec(memory_space=pltpu.SMEM)
     vmem = pl.BlockSpec(memory_space=pltpu.VMEM)
-    whole = pl.BlockSpec(memory_space=pl.ANY)
+    whole = pl.BlockSpec(memory_space=pltpu.HBM)
     half = jnp.bfloat16
     dma = pltpu.SemaphoreType.DMA
     carried, output = pl.pallas_call(
@@ -646,18 +652,20 @@
             jax.ShapeDtypeStruct(residual.shape, half),
             jax.ShapeDtypeStruct(residual.shape, half),
         ),
-        in_specs=[smem, smem, whole, whole, vmem, vmem, whole, whole, whole, whole],
+        in_specs=[smem, smem, whole, whole, whole, whole, whole, whole, whole, whole],
         out_specs=(vmem, vmem),
         scratch_shapes=[
             pltpu.VMEM((ROWS, features), half),
             pltpu.VMEM((ROWS, features), half),
+            pltpu.VMEM((1, features), half),
+            pltpu.VMEM((8, HD), jnp.float32),
             pltpu.VMEM((features, query_width), half),
             pltpu.VMEM((features, pair_width), half),
             pltpu.VMEM((query_width, features), half),
             pltpu.VMEM((PREFIX, HD), half),
-            pltpu.VMEM((PREFIX, HD), half),
+            pltpu.VMEM((PREFIX, 2 * HD), half),
             pltpu.VMEM((2, SPAN, HD), half),
-            pltpu.VMEM((2, SPAN, HD), half),
+            pltpu.VMEM((2, SPAN, 2 * HD), half),
             pltpu.VMEM((2 * SPAN, features), half),
             pltpu.VMEM((ROWS, features), half),
             pltpu.VMEM((ROWS, features), half),
@@ -668,8 +676,7 @@
             pltpu.VMEM((SPAN, query_width + pair_width), jnp.float32),
             pltpu.VMEM((4, query_width // HD * HALF, HD), half),
             pltpu.VMEM((2, query_width // HD * HALF, HD), jnp.float32),
-            pltpu.VMEM((2, query_width // HD * HALF, HD), jnp.float32),
-            pltpu.VMEM((2, query_width // HD * HALF, HD), jnp.float32),
+            pltpu.VMEM((2, query_width // HD * HALF, 2 * HD), jnp.float32),
             pltpu.VMEM((SPAN, query_width), half),
             pltpu.VMEM((SPAN, features), jnp.float32),
             pltpu.VMEM((2, OUT_CHUNKS, 2, ROWS, chunk), half),
@@ -678,7 +685,7 @@
             pltpu.VMEM((2, OUT_CHUNKS, ROWS, chunk), half),
             pltpu.VMEM((OUT_CHUNKS, ROWS, chunk), half),
             pltpu.VMEM((OUT_CHUNKS, ROWS, chunk), half),
-            dma((2,)),
+            dma((4,)),
             dma((11,)),
             dma((2, 3, 2)),
             dma((2, 3, 2)),
@@ -692,7 +699,7 @@
             dma((OUT_CHUNKS,)),
         ],
         compiler_params=pltpu.CompilerParams(
-            collective_id=0, has_side_effects=True, vmem_limit_bytes=46 * 1024 * 1024
+            collective_id=0, has_side_effects=True, vmem_limit_bytes=60 * 1024 * 1024
         ),
         name="fused_relay",
     )(

time: 44.1 us -> 59.1 us (1.34); the launches traced: 43.2 us -> 59 us
  Pallas kernels: 35.1 us -> 56.9 us
  local copies, waits for them, and re-layouts: 6.02 us -> 0 us
    pallas_call x1, Pallas kernels: 0.82 us -> 17 us  [hand_out(): pl.pallas_call(hand_out_kernel, out_shape=(shape, shape), in_specs=[whole...]
    unnamed x12 -> x0, local copies, waits for them, and re-layouts: 6.02 us -> none
    pallas_call x1, Pallas kernels: 34.3 us -> 39.9 us  [fused(): pl.pallas_call(functools.partial(fused_kernel, sections), out_shape=(jax....]
where the time goes in v3:
time: 59.1 us; the launch traced here: 59 us
  Pallas kernels  56.9 us (96%)
  between operations  2.09 us (4%)
    pallas_call x1, Pallas kernels, fused(): pl.pallas_call(functools.partial(fused_kernel, sections), out_shape=(jax....  39.9 us
    pallas_call x1, Pallas kernels, hand_out(): pl.pallas_call(hand_out_kernel, out_shape=(shape, shape), in_specs=[whole...  17 us

profile of v3, /device:TPU:0, one launch (start us, length us, event | category | flops | bytes accessed | tf_op | source)
XLA Modules:
  0.0 59.0 jit_solution(10275037126349160247)
XLA Ops:
  1.9 39.9 %fused_relay.1 = (bf16[1,32,4096]{2,1,0:T(8,128)(2,1)}, bf16[1,32,4096]{2,1,0:T(8,128)(2,1)}) custom-call(s32[1]{0:T(128)S(6)} %copy.12.span_ref, s32[1]{0:T(128)S(6)} %copy.13.len_ref, bf16[1,32,4096]{2,1,0:T(8,128)(2,1)} %residual_hbm.1, bf16[1,32,4096]{2,1,0:T(8,128)(2,1)} %pending_hbm.1, bf16[1,4096]{1,0:T(2,128)(2,1)} %gain_hbm.1, ...), custom_call_target="tpu_custom_call" | custom-call | tf_op jit(solution)/shard_map/fused_relay/pallas_call | solution.py:649
  41.8 17.0 %hand_out.1 = (bf16[1,32,4096]{2,1,0:T(8,128)(2,1)}, bf16[1,32,4096]{2,1,0:T(8,128)(2,1)}) custom-call(bf16[1,32,4096]{2,1,0:T(8,128)(2,1)} %get-tuple-element.4.carried_from, bf16[1,32,4096]{2,1,0:T(8,128)(2,1)} %get-tuple-element.5.output_from), custom_call_target="tpu_custom_call" | custom-call | tf_op jit(solution)/shard_map/hand_out/pallas_call | solution.py:615

commit v4 on v2

--- a/solution.py
+++ b/solution.py
@@ -168,8 +168,7 @@
     len_ref,
     residual_hbm,
     pending_hbm,
-    gain_ref,
-    inverse_ref,
+    gain_hbm,
     w_query_hbm,
     w_kv_hbm,
     w_out_hbm,
@@ -178,6 +177,7 @@
     output_ref,
     residual,
     pending,
+    gain_ref,
     w_query,
     w_kv,
     w_out,
@@ -245,6 +245,7 @@
 
     row_loads = [
         pltpu.make_async_copy(residual_hbm.at[0], residual, row_sem.at[0]),
+        pltpu.make_async_copy(gain_hbm, gain_ref, row_sem.at[2]),
         pltpu.make_async_copy(pending_hbm.at[0], pending, row_sem.at[1]),
     ]
     loads = []
@@ -263,10 +264,8 @@
         pltpu.make_async_copy(source, target, load_sem.at[number])
         for number, (source, target) in enumerate(loads)
     ]
-    for load in row_loads + loads:
+    for load in row_loads:
         load.start()
-
-    gain = gain_ref[...].astype(jnp.float32)
 
     def rows_of(slot, which, part=None):
         if part is None:
@@ -275,6 +274,7 @@
 
     def normed(rows):
         widths = rows.astype(jnp.float32)
+        gain = gain_ref[...].astype(jnp.float32)
         mean_square = jnp.mean(widths * widths, axis=-1, keepdims=True)
         return (widths * lax.rsqrt(mean_square + norm_eps) * gain).astype(jnp.bfloat16)
 
@@ -335,8 +335,11 @@
         )
 
     row_loads[0].wait()
+    row_loads[1].wait()
+    for load in loads:
+        load.start()
     tokens[rows_of(0, core)] = normed(residual[...])
-    row_loads[1].wait()
+    row_loads[2].wait()
     carried_own[...] = (
         residual[...].astype(jnp.float32) + pending[...].astype(jnp.float32)
     ).astype(jnp.bfloat16)
@@ -364,11 +367,15 @@
 
     lane = lax.broadcasted_iota(jnp.int32, (SPAN, HD), 1)
     token = (lax.broadcasted_iota(jnp.int32, (SPAN, HD), 0) + side * HALF) & (SPAN - 1)
+    inverse = jnp.zeros((1, HD), jnp.float32)
+    frequencies = (rope_base ** (-np.arange(0, HD, 2, dtype=np.float64) / HD)).astype(np.float32)
+    for place, frequency in enumerate(frequencies):
+        inverse = jnp.where(lane[0:1] % (HD // 2) == place, float(frequency), inverse)
     key_token = (lane + side * HALF) & (SPAN - 1)
 
     def tables(tick, index_tile):
         positions = (index_tile[0:1, :] * SPAN + token).astype(jnp.float32)
-        angles = positions * inverse_ref[0:1, :]
+        angles = positions * inverse
         sine = jnp.sin(angles)
         cosines[tick] = jnp.cos(angles)
         sines[tick] = jnp.where(lane < HD // 2, -sine, sine)
@@ -457,10 +464,11 @@
             peak = jnp.maximum(before, jnp.max(scores, axis=-1, keepdims=True))
             weights = jnp.exp2(scores - peak)
             shrink = jnp.exp2(before - peak)
-            total = totals[half, rows] * shrink + jnp.sum(weights, axis=-1, keepdims=True)
-            mixed = mixes[half, rows] * shrink + jnp.dot(
+            fresh = jnp.dot(
                 weights.astype(jnp.bfloat16), span_values[tick], preferred_element_type=jnp.float32
             )
+            total = totals[half, rows] * shrink + jnp.sum(weights, axis=-1, keepdims=True)
+            mixed = mixes[half, rows] * shrink + fresh
             mixed = (mixed / total).astype(jnp.bfloat16)
             for place in range(group):
                 head = block * group + place
@@ -488,10 +496,11 @@
                     jnp.bfloat16
                 )
                 pair_copy(tick, number, kind).start()
-            if 1 in halves and number > 0:
-                pass_on(tick, number - 1)
+            if 1 in halves and number > 1:
+                pass_on(tick, number - 2)
         if 1 in halves:
-            pass_on(tick, OUT_CHUNKS - 1)
+            for number in range(OUT_CHUNKS - 2, OUT_CHUNKS):
+                pass_on(tick, number)
 
     def summed(tick, number):
         columns = slice(number * chunk, (number + 1) * chunk)
@@ -546,8 +555,10 @@
     spread((3,))
     attend_prefix(3)
     attend_span(3)
+    for number in range(OUT_CHUNKS // 2):
+        finish_first(number)
     emit(1, (1,))
-    for number in range(OUT_CHUNKS):
+    for number in range(OUT_CHUNKS // 2, OUT_CHUNKS):
         finish_first(number)
     attend_prefix(2)
     attend_span(2)
@@ -604,15 +615,16 @@
 
 
 def hand_out(carried, output):
+    near = pl.BlockSpec(memory_space=pltpu.VMEM)
     whole = pl.BlockSpec(memory_space=pl.ANY)
     shape = jax.ShapeDtypeStruct(carried.shape, carried.dtype)
     return pl.pallas_call(
         hand_out_kernel,
         out_shape=(shape, shape),
-        in_specs=[whole, whole],
+        in_specs=[near, near],
         out_specs=(whole, whole),
         scratch_shapes=[pltpu.SemaphoreType.DMA((2, 2))],
-        compiler_params=pltpu.CompilerParams(vmem_limit_bytes=1024 * 1024),
+        compiler_params=pltpu.CompilerParams(vmem_limit_bytes=4 * 1024 * 1024),
         name="hand_out",
     )(carried, output)
 
@@ -632,9 +644,6 @@
     features, query_width = w_query.shape[1:]
     pair_width = w_kv.shape[2]
     chunk = features // OUT_CHUNKS
-    exponents = -np.arange(0, HD, 2, dtype=np.float64) / HD
-    inverse = np.tile((rope_base**exponents).astype(np.float32), 2)
-    inverse = jnp.asarray(np.tile(inverse[None], (8, 1)))
     smem = pl.BlockSpec(memory_space=pltpu.SMEM)
     vmem = pl.BlockSpec(memory_space=pltpu.VMEM)
     whole = pl.BlockSpec(memory_space=pl.ANY)
@@ -646,11 +655,12 @@
             jax.ShapeDtypeStruct(residual.shape, half),
             jax.ShapeDtypeStruct(residual.shape, half),
         ),
-        in_specs=[smem, smem, whole, whole, vmem, vmem, whole, whole, whole, whole],
+        in_specs=[smem, smem] + [whole] * 7,
         out_specs=(vmem, vmem),
         scratch_shapes=[
             pltpu.VMEM((ROWS, features), half),
             pltpu.VMEM((ROWS, features), half),
+            pltpu.VMEM((1, features), half),
             pltpu.VMEM((features, query_width), half),
             pltpu.VMEM((features, pair_width), half),
             pltpu.VMEM((query_width, features), half),
@@ -678,7 +688,7 @@
             pltpu.VMEM((2, OUT_CHUNKS, ROWS, chunk), half),
             pltpu.VMEM((OUT_CHUNKS, ROWS, chunk), half),
             pltpu.VMEM((OUT_CHUNKS, ROWS, chunk), half),
-            dma((2,)),
+            dma((3,)),
             dma((11,)),
             dma((2, 3, 2)),
             dma((2, 3, 2)),
@@ -692,7 +702,7 @@
             dma((OUT_CHUNKS,)),
         ],
         compiler_params=pltpu.CompilerParams(
-            collective_id=0, has_side_effects=True, vmem_limit_bytes=46 * 1024 * 1024
+            collective_id=0, has_side_effects=True, vmem_limit_bytes=54528 * 1024
         ),
         name="fused_relay",
     )(
@@ -701,7 +711,6 @@
         residual,
         pending,
         norm_gain,
-        inverse,
         w_query,
         w_kv,
         w_out,

time: 44.1 us -> 37.7 us (0.85); the launches traced: 43.2 us -> 37.4 us
  local copies, waits for them, and re-layouts: 6.02 us -> 0.71 us
  Pallas kernels: 35.1 us -> 34.6 us
    unnamed x12 -> x2, local copies, waits for them, and re-layouts: 6.02 us -> 0.71 us
    pallas_call x1, Pallas kernels: 34.3 us -> 33.8 us  [fused(): pl.pallas_call(functools.partial(fused_kernel, sections), out_shape=(jax....]
where the time goes in v4:
time: 37.7 us; the launch traced here: 37.4 us
  Pallas kernels  34.6 us (92%)
  between operations  2.1 us (6%)
  local copies, waits for them, and re-layouts  0.71 us (2%)
    pallas_call x1, Pallas kernels, fused(): pl.pallas_call(functools.partial(fused_kernel, sections), out_shape=(jax....  33.8 us
    pallas_call x1, Pallas kernels, hand_out(): pl.pallas_call(hand_out_kernel, out_shape=(shape, shape), in_specs=[near,...  0.82 us

profile of v4, /device:TPU:0, one launch (start us, length us, event | category | flops | bytes accessed | tf_op | source)
XLA Modules:
  0.0 37.4 jit_solution(5848274339930670088)
XLA Ops:
  1.9 0.0 copy-start
  1.9 0.7 %copy-done = bf16[1,4096]{1,0:T(2,128)(2,1)S(1)} copy-done((bf16[1,4096]{1,0:T(2,128)(2,1)S(1)}, bf16[1,4096]{1,0:T(2,128)(2,1)}, u32[]{:S(2)}) %copy-start) | copy-done | bytes 8216
  2.6 33.8 %fused_relay.1 = (bf16[1,32,4096]{2,1,0:T(8,128)(2,1)S(1)}, bf16[1,32,4096]{2,1,0:T(8,128)(2,1)S(1)}) custom-call(s32[1]{0:T(128)S(6)} %copy.11.span_ref, s32[1]{0:T(128)S(6)} %copy.12.len_ref, bf16[1,32,4096]{2,1,0:T(8,128)(2,1)} %residual_hbm.1, bf16[1,32,4096]{2,1,0:T(8,128)(2,1)} %pending_hbm.1, bf16[1,4096]{1,0:T(2,128)(2,1)S(1)} %copy-done, ...), custom_call_target="tpu_custom_call" | custom-call | tf_op jit(solution)/shard_map/fused_relay/pallas_call | solution.py:652
  36.5 0.8 %hand_out.1 = (bf16[1,32,4096]{2,1,0:T(8,128)(2,1)}, bf16[1,32,4096]{2,1,0:T(8,128)(2,1)}) custom-call(bf16[1,32,4096]{2,1,0:T(8,128)(2,1)S(1)} %get-tuple-element.4.carried_from, bf16[1,32,4096]{2,1,0:T(8,128)(2,1)S(1)} %get-tuple-element.5.output_from), custom_call_target="tpu_custom_call" | custom-call | tf_op jit(solution)/shard_map/hand_out/pallas_call | solution.py:621
Async XLA Ops:
  1.9 0.7 %copy-start = (bf16[1,4096]{1,0:T(2,128)(2,1)S(1)}, bf16[1,4096]{1,0:T(2,128)(2,1)}, u32[]{:S(2)}) copy-start(bf16[1,4096]{1,0:T(2,128)(2,1)} %gain_hbm.1) | copy-start | bytes 24580

commit v5 on v4

--- a/solution.py
+++ b/solution.py
@@ -336,20 +336,19 @@
 
     row_loads[0].wait()
     row_loads[1].wait()
-    for load in loads:
+    for load in loads[:5]:
         load.start()
-    tokens[rows_of(0, core)] = normed(residual[...])
+    for part in range(2):
+        tokens[rows_of(0, core, part)] = normed(residual[part * PIECE : (part + 1) * PIECE])
+        if part == 0:
+            pl.semaphore_wait(barrier, 2 + has_prev.astype(jnp.int32) + has_next.astype(jnp.int32))
+        gather_copy(0, 0, part).start()
     row_loads[2].wait()
     carried_own[...] = (
         residual[...].astype(jnp.float32) + pending[...].astype(jnp.float32)
     ).astype(jnp.bfloat16)
     index_own[...] = jnp.full(index_own.shape, span_ref[0], jnp.int32)
 
-    pl.semaphore_wait(barrier, 2 + has_prev.astype(jnp.int32) + has_next.astype(jnp.int32))
-
-    for part in range(2):
-        gather_copy(0, 0, part).start()
-
     @pl.when(has_next)
     def _():
         for part in range(2):
@@ -358,6 +357,8 @@
 
     for part in range(2):
         gather_copy(0, 1, part).start()
+    for load in loads[5:]:
+        load.start()
 
     @pl.when(jnp.logical_not(has_prev))
     def _():
@@ -393,10 +394,11 @@
     score_scale = HD ** (-0.5) * math.log2(math.e)
     transposed = (((1,), (1,)), ((), ()))
 
-    def relay_and_shift(part):
-        gather_copy(0, 0, part).wait_recv()
-        gather_copy(0, 2, part).start()
-
+    def relay(tick, part):
+        gather_copy(tick, 0, part).wait_recv()
+        gather_copy(tick, 2, part).start()
+
+    def take_shifted(part):
         @pl.when(has_prev)
         def _():
             shift_copy(part).wait_recv()
@@ -522,37 +524,37 @@
     for load in loads[:5]:
         load.wait()
     project((0,))
-    relay_and_shift(0)
+    relay(0, 0)
     spread((0,))
     for load in loads[5:7]:
         load.wait()
     attend_prefix(0)
-    relay_and_shift(1)
-
-    @pl.when(has_prev)
-    def _():
-        index_copy().wait_recv()
-
-    tables(1, index_in[...])
+    relay(0, 1)
+    take_shifted(0)
     for part in range(2):
         gather_copy(0, 2, part).wait_recv()
-        gather_copy(1, 1, part).wait_recv()
-    project((1, 2))
-    spread((1, 2))
+    project((1,))
+    take_shifted(1)
+    spread((1,))
     attend_prefix(1)
     attend_span(1)
     attend_span(0)
     for load in loads[7:]:
         load.wait()
     for part in range(2):
-        gather_copy(1, 0, part).wait_recv()
-        gather_copy(1, 2, part).start()
+        relay(1, part)
     emit(0, (0, 1))
 
+    @pl.when(has_prev)
+    def _():
+        index_copy().wait_recv()
+
+    tables(1, index_in[...])
     for part in range(2):
+        gather_copy(1, 1, part).wait_recv()
         gather_copy(1, 2, part).wait_recv()
-    project((3,))
-    spread((3,))
+    project((2, 3))
+    spread((2, 3))
     attend_prefix(3)
     attend_span(3)
     for number in range(OUT_CHUNKS // 2):

time: 37.7 us -> 40.7 us (1.080)
  Pallas kernels: 34.6 us -> 37.6 us
    pallas_call x1, Pallas kernels: 33.8 us -> 36.8 us  [fused(): pl.pallas_call(functools.partial(fused_kernel, sections), out_shape=(jax....]
where the time goes in v5:
time: 40.7 us; the launch traced here: 40.5 us
  Pallas kernels  37.6 us (92%)
  between operations  2.1 us (5%)
  local copies, waits for them, and re-layouts  0.71 us (2%)
    pallas_call x1, Pallas kernels, fused(): pl.pallas_call(functools.partial(fused_kernel, sections), out_shape=(jax....  36.8 us
    pallas_call x1, Pallas kernels, hand_out(): pl.pallas_call(hand_out_kernel, out_shape=(shape, shape), in_specs=[near,...  0.82 us

profile of v5, /device:TPU:0, one launch (start us, length us, event | category | flops | bytes accessed | tf_op | source)
XLA Modules:
  0.0 40.5 jit_solution(9167783750577843648)
XLA Ops:
  1.9 0.0 copy-start
  1.9 0.7 %copy-done = bf16[1,4096]{1,0:T(2,128)(2,1)S(1)} copy-done((bf16[1,4096]{1,0:T(2,128)(2,1)S(1)}, bf16[1,4096]{1,0:T(2,128)(2,1)}, u32[]{:S(2)}) %copy-start) | copy-done | bytes 8216
  2.6 36.8 %fused_relay.1 = (bf16[1,32,4096]{2,1,0:T(8,128)(2,1)S(1)}, bf16[1,32,4096]{2,1,0:T(8,128)(2,1)S(1)}) custom-call(s32[1]{0:T(128)S(6)} %copy.11.span_ref, s32[1]{0:T(128)S(6)} %copy.12.len_ref, bf16[1,32,4096]{2,1,0:T(8,128)(2,1)} %residual_hbm.1, bf16[1,32,4096]{2,1,0:T(8,128)(2,1)} %pending_hbm.1, bf16[1,4096]{1,0:T(2,128)(2,1)S(1)} %copy-done, ...), custom_call_target="tpu_custom_call" | custom-call | tf_op jit(solution)/shard_map/fused_relay/pallas_call | solution.py:654
  39.5 0.8 %hand_out.1 = (bf16[1,32,4096]{2,1,0:T(8,128)(2,1)}, bf16[1,32,4096]{2,1,0:T(8,128)(2,1)}) custom-call(bf16[1,32,4096]{2,1,0:T(8,128)(2,1)S(1)} %get-tuple-element.4.carried_from, bf16[1,32,4096]{2,1,0:T(8,128)(2,1)S(1)} %get-tuple-element.5.output_from), custom_call_target="tpu_custom_call" | custom-call | tf_op jit(solution)/shard_map/hand_out/pallas_call | solution.py:623
Async XLA Ops:
  1.9 0.7 %copy-start = (bf16[1,4096]{1,0:T(2,128)(2,1)S(1)}, bf16[1,4096]{1,0:T(2,128)(2,1)}, u32[]{:S(2)}) copy-start(bf16[1,4096]{1,0:T(2,128)(2,1)} %gain_hbm.1) | copy-start | bytes 24580

commit v6 on v4

--- a/solution.py
+++ b/solution.py
@@ -338,17 +338,16 @@
     row_loads[1].wait()
     for load in loads:
         load.start()
-    tokens[rows_of(0, core)] = normed(residual[...])
+    for part in range(2):
+        tokens[rows_of(0, core, part)] = normed(residual[part * PIECE : (part + 1) * PIECE])
+        if part == 0:
+            pl.semaphore_wait(barrier, 2 + has_prev.astype(jnp.int32) + has_next.astype(jnp.int32))
+        gather_copy(0, 0, part).start()
     row_loads[2].wait()
     carried_own[...] = (
         residual[...].astype(jnp.float32) + pending[...].astype(jnp.float32)
     ).astype(jnp.bfloat16)
     index_own[...] = jnp.full(index_own.shape, span_ref[0], jnp.int32)
-
-    pl.semaphore_wait(barrier, 2 + has_prev.astype(jnp.int32) + has_next.astype(jnp.int32))
-
-    for part in range(2):
-        gather_copy(0, 0, part).start()
 
     @pl.when(has_next)
     def _():

time: 37.7 us -> 37.7 us (level)
  no operation moved by 1% of the time
where the time goes in v6:
time: 37.7 us; the launch traced here: 37.4 us
  Pallas kernels  34.6 us (92%)
  between operations  2.1 us (6%)
  local copies, waits for them, and re-layouts  0.71 us (2%)
    pallas_call x1, Pallas kernels, fused(): pl.pallas_call(functools.partial(fused_kernel, sections), out_shape=(jax....  33.8 us
    pallas_call x1, Pallas kernels, hand_out(): pl.pallas_call(hand_out_kernel, out_shape=(shape, shape), in_specs=[near,...  0.82 us

profile of v6, /device:TPU:0, one launch (start us, length us, event | category | flops | bytes accessed | tf_op | source)
XLA Modules:
  0.0 37.4 jit_solution(8119026734342836642)
XLA Ops:
  1.9 0.0 copy-start
  1.9 0.7 %copy-done = bf16[1,4096]{1,0:T(2,128)(2,1)S(1)} copy-done((bf16[1,4096]{1,0:T(2,128)(2,1)S(1)}, bf16[1,4096]{1,0:T(2,128)(2,1)}, u32[]{:S(2)}) %copy-start) | copy-done | bytes 8216
  2.6 33.8 %fused_relay.1 = (bf16[1,32,4096]{2,1,0:T(8,128)(2,1)S(1)}, bf16[1,32,4096]{2,1,0:T(8,128)(2,1)S(1)}) custom-call(s32[1]{0:T(128)S(6)} %copy.11.span_ref, s32[1]{0:T(128)S(6)} %copy.12.len_ref, bf16[1,32,4096]{2,1,0:T(8,128)(2,1)} %residual_hbm.1, bf16[1,32,4096]{2,1,0:T(8,128)(2,1)} %pending_hbm.1, bf16[1,4096]{1,0:T(2,128)(2,1)S(1)} %copy-done, ...), custom_call_target="tpu_custom_call" | custom-call | tf_op jit(solution)/shard_map/fused_relay/pallas_call | solution.py:651
  36.5 0.8 %hand_out.1 = (bf16[1,32,4096]{2,1,0:T(8,128)(2,1)}, bf16[1,32,4096]{2,1,0:T(8,128)(2,1)}) custom-call(bf16[1,32,4096]{2,1,0:T(8,128)(2,1)S(1)} %get-tuple-element.4.carried_from, bf16[1,32,4096]{2,1,0:T(8,128)(2,1)S(1)} %get-tuple-element.5.output_from), custom_call_target="tpu_custom_call" | custom-call | tf_op jit(solution)/shard_map/hand_out/pallas_call | solution.py:620
Async XLA Ops:
  1.9 0.7 %copy-start = (bf16[1,4096]{1,0:T(2,128)(2,1)S(1)}, bf16[1,4096]{1,0:T(2,128)(2,1)}, u32[]{:S(2)}) copy-start(bf16[1,4096]{1,0:T(2,128)(2,1)} %gain_hbm.1) | copy-start | bytes 24580
